TPU v7x, 32 devices: a whole 2x2x4 slice. The times are simulated.
32 devices in a mesh: rows: 16 (over z, y, x), hid: 2 (over core).
Axes of the slice: x: 2, y: 2, z: 4, core: 2. Of those that a mesh axis runs over, the one named last changes fastest.
Arguments:
- hidden_in: bfloat16 [4096, 768], P('rows', 'hid'), may hold values from -6 to 6
- d_out: bfloat16 [4096, 768], P('rows', 'hid'), may hold values from -6 to 6
- gains: float32 [2, 2, 768], P(None, None, 'hid'), may hold values from 0.25 to 1.75
- mixer: bfloat16 [2, 3, 4, 192, 192], P(None, None, 'hid'), may hold values from -0.4375 to 0.4375
- skip: float32 [2, 768], P(None, 'hid'), may hold values from -3 to 3
- filters: float32 [2, 2, 128, 768], P(None, None, None, 'hid'), may hold values from -0.5 to 0.5
- gate_up: bfloat16 [2, 2, 768, 3072], P(None, None, None, 'hid'), may hold values from -0.21875 to 0.21875
- down: bfloat16 [2, 768, 3072], P(None, None, 'hid'), may hold values from -0.109375 to 0.109375
Outputs:
- hidden_out: bfloat16 [4096, 768], P('rows', 'hid')
- grad_in: float32 [4096, 768], P('rows', 'hid')
- grad_gains: float32 [2, 2, 768], P(None, None, 'hid')
- grad_mixer: float32 [2, 3, 4, 192, 192], P(None, None, 'hid')
- grad_skip: float32 [2, 768], P(None, 'hid')
- grad_filters: float32 [2, 2, 128, 768], P(None, None, None, 'hid')
- grad_gate_up: float32 [2, 2, 768, 3072], P(None, None, 'rows', 'hid')
- grad_down: float32 [2, 768, 3072], P(None, 'rows', 'hid')
All inputs are finite; a program needn't handle non-finite values.
Results may differ from a plain program's by a relative error of at most 0.019.
Values may be sent and summed in bfloat16 or wider, within the bound.
A program may use at most 192 MiB of HBM per device.

v0:
```python
import functools
import math

import jax
import jax.numpy as jnp
import numpy as np
from jax import lax
from jax.experimental import pallas as pl
from jax.experimental.pallas import tpu as pltpu
from jax.sharding import PartitionSpec as P

ORDER = 128
SEQ_LEN = 8192
LANES = 128
NORM_EPS = 1e-05
DECAY = 0.02
MESH = pl.DeviceIdType.MESH
BF16 = jnp.bfloat16
F32 = jnp.float32
MIB = 2**20
GELU_C = math.sqrt(2.0 / math.pi)


def round_up(value, step):
    return -(-value // step) * step


def whole():
    return pl.BlockSpec(memory_space=pltpu.VMEM)


def nn(a, b):
    return lax.dot_general(a, b, (((1,), (0,)), ((), ())), preferred_element_type=F32)


def nt(a, b):
    return lax.dot_general(a, b, (((1,), (1,)), ((), ())), preferred_element_type=F32)


def tn(a, b):
    return lax.dot_general(a, b, (((0,), (0,)), ((), ())), preferred_element_type=F32)


def position_table(length):
    half_order = ORDER // 2
    index_list = np.arange(half_order)
    multiple = 1 + index_list * index_list * (length // 4) // (half_order * half_order)
    phase = (np.arange(length)[:, None] * multiple[None, :] % length) * (2.0 * math.pi / length)
    return np.concatenate([np.sin(phase), np.cos(phase)], axis=1)


def dft_tables(length):
    blocks = length // LANES
    size = 2 * length
    outer = 2 * blocks
    k = np.arange(outer)
    n = np.arange(blocks)
    m = np.arange(LANES)
    angle = 2.0 * math.pi * (np.outer(k, n) % outer) / outer
    outer_fwd = np.concatenate([np.cos(angle), -np.sin(angle)], axis=0)
    outer_inv = np.concatenate([np.cos(angle), -np.sin(angle)], axis=0).T / size
    angle = 2.0 * math.pi * (np.outer(m, m) % LANES) / LANES
    cos, sin = np.cos(angle), np.sin(angle)
    inner_fwd = np.block([[cos, -sin], [sin, cos]])
    inner_inv = np.block([[cos, sin], [-sin, cos]])
    angle = 2.0 * math.pi * np.outer(k, m) / size
    twist = np.concatenate([np.cos(angle), np.sin(angle)], axis=1)
    half = lambda table: jnp.asarray(table, F32).astype(BF16)
    return (half(outer_fwd), half(outer_inv), half(inner_fwd), half(inner_inv), jnp.asarray(twist, F32))


def normalize(values):
    mean = jnp.mean(values, axis=1, keepdims=True)
    square = jnp.mean(values * values, axis=1, keepdims=True)
    inv = lax.rsqrt(square - mean * mean + NORM_EPS)
    return (values - mean) * inv, inv


def norm_back(grad, normal, inv, gain):
    scaled = grad * gain
    mean = jnp.mean(scaled, axis=1, keepdims=True)
    cross = jnp.mean(scaled * normal, axis=1, keepdims=True)
    return inv * (scaled - mean - normal * cross), jnp.sum(grad * normal, axis=0, keepdims=True)


def gelu_parts(gate):
    square = gate * gate
    tanh = jnp.tanh(GELU_C * gate * (1.0 + 0.044715 * square))
    half = 0.5 * (1.0 + tanh)
    value = gate * half
    slope = half + 0.5 * gate * (1.0 - tanh * tanh) * (GELU_C * (1.0 + 3.0 * 0.044715 * square))
    return value, slope


class Sizes:
    def __init__(self, rows, hid, tokens, width, hidden, layers, blocks):
        self.rows, self.hid, self.width, self.layers = rows, hid, width, layers
        self.count = rows * hid
        self.own = tokens // self.count
        self.half = width // hid
        self.units = hidden // hid
        self.blocks = blocks
        self.size = width // blocks
        self.side_blocks = blocks // hid
        self.couple = 2 * width // self.count
        self.big = round_up(self.couple // 2, 16)
        self.small = self.couple - self.big
        self.length = min(SEQ_LEN, tokens)
        self.seqs = tokens // self.length
        self.steps = self.length // LANES
        self.outer = 2 * self.steps
        self.pairs = self.seqs * self.big
        self.group = 4
        self.peers = rows // self.group
        self.part = self.units // self.group
        self.depth = width // rows
        self.deep = round_up(self.depth, 16)
        self.deeps = tuple(
            round_up(-(-rows_needed // rows), 16)
            for rows_needed in (3 * (layers - 1) * self.size, 2 * self.size + 16)
        )
        self.late_rows = round_up(-(-(self.size + 16) // rows), 16)
        self.taps_rows = round_up(2 * self.big + 1, 16)


    @classmethod
    def of(cls, hidden_in, d_out, gains, mixer, skip, filters, gate_up, down):
        rows, hid = lax.axis_size("rows"), lax.axis_size("hid")
        layers, _, width, units = gate_up.shape
        tokens = hidden_in.shape[0] * rows
        return cls(rows, hid, tokens, width, units * hid, layers, mixer.shape[2] * hid)


    def fits(self):
        whole_tiles = self.small > 0 and self.small % 16 == 0 and self.rows % 8 == 0
        whole_tiles = whole_tiles and self.own == LANES and self.depth % 16 == 0
        whole_tiles = whole_tiles and self.peers == 4 and self.layers == 2 and self.seqs == 1
        whole_tiles = whole_tiles and all(self.size % deep == 0 for deep in self.deeps)
        total = 0
        for spec in layout(self)[1]:
            size = jnp.dtype(spec.dtype).itemsize
            *lead, rows, lanes = spec.shape
            total += math.prod(lead) * round_up(rows, 32 // size) * round_up(lanes, LANES) * size
        return whole_tiles and total <= 60 * MIB


class Links:
    def __init__(self, sz, sems, local_sems):
        self.sz, self.sems, self.local_sems = sz, sems, local_sems
        self.used = 0
        self.used_local = 0
        self.row = lax.axis_index("rows")
        self.col = lax.axis_index("hid")
        self.plane = lax.rem(self.row, sz.peers)
        self.line = self.row // sz.peers

    def pair(self):
        first = self.used
        self.used += 2
        return self.sems.at[first], self.sems.at[first + 1]

    def copy(self, source, target, pair, row, col):
        return pltpu.make_async_remote_copy(
            src_ref=source,
            dst_ref=target,
            send_sem=pair[0],
            recv_sem=pair[1],
            device_id=(row, col),
            device_id_type=MESH,
        )

    def sibling(self, source, target):
        copy = self.copy(source, target, self.pair(), self.row, self.sz.hid - 1 - self.col)
        copy.start()
        return copy

    def load(self, source, target):
        copy = pltpu.make_async_copy(source, target, self.local_sems.at[self.used_local])
        self.used_local += 1
        copy.start()
        return copy

    def groups(self, count, me, row_of, source_of, target):
        pair = self.pair()

        def post(step, carry):
            member = lax.rem(me + step, count)
            self.copy(source_of(member), target, pair, row_of(member), self.col).start()
            return carry

        lax.fori_loop(1, count, post, 0)
        return pair

    def in_plane(self, source_of, target):
        row_of = lambda member: self.line * self.sz.peers + member
        return self.groups(self.sz.peers, self.plane, row_of, source_of, target)

    def in_line(self, source_of, target):
        row_of = lambda member: member * self.sz.peers + self.plane
        return self.groups(self.sz.group, self.line, row_of, source_of, target)

    def in_rows(self, source_of, target):
        return self.groups(self.sz.rows, self.row, lambda member: member, source_of, target)

    def wait(self, pair, span):
        self.copy(span, span, pair, self.row, self.sz.hid - 1 - self.col).wait()


class Plane:
    def __init__(self, links):
        self.links = links
        self.me = links.plane
        along_x = self.me + 1 - 2 * lax.rem(self.me, 2)
        along_y = self.me + 2 - 4 * (self.me // 2)
        self.near = (along_x, along_y)
        self.far = (along_y, along_x)
        self.across = 3 - self.me

    def send(self, copies):
        links = self.links
        pair = links.pair()
        for source, target, member in copies:
            row = links.line * links.sz.peers + member
            links.copy(source, target, pair, row, links.col).start()
        return pair


class PlaneSum(Plane):
    def __init__(self, links, source, first, give, second):
        super().__init__(links)
        self.source, self.first, self.give, self.second = source, first, give, second

    def start(self):
        copies = []
        for half in range(2):
            for which, member in enumerate((self.near[half], self.across)):
                target = self.first.at[half, which]
                copies.append((self.source(member, half), target, self.near[half]))
        self.pair = self.send(copies)

    def middle(self):
        self.links.wait(self.pair, self.first)
        copies = []
        for half in range(2):
            theirs = self.source(self.far[half], half)[...].astype(F32)
            self.give[half] = (theirs + self.first[half, 1].astype(F32)).astype(BF16)
            mine = self.source(self.me, half)[...].astype(F32)
            self.first[half, 0] = (mine + self.first[half, 0].astype(F32)).astype(BF16)
            copies.append((self.give.at[half], self.second.at[half], self.far[half]))
        self.pair = self.send(copies)

    def end(self):
        self.links.wait(self.pair, self.second)

    def sums(self):
        for half in range(2):
            total = self.first[half, 0].astype(F32) + self.second[half].astype(F32)
            self.second[half] = total.astype(BF16)
        count = self.links.sz.group // 2
        return lambda member: self.second.at[member // count, lax.rem(member, count)]


class PlaneSpread(Plane):
    def __init__(self, links, place, span):
        super().__init__(links)
        self.place, self.span = place, span

    def start(self):
        copies = []
        for half in range(2):
            here = self.place(self.me, half)
            copies.append((here, here, self.near[half]))
        self.pair = self.send(copies)

    def middle(self):
        self.links.wait(self.pair, self.span(1))
        copies = []
        for half in range(2):
            for member in (self.me, self.near[half]):
                here = self.place(member, half)
                copies.append((here, here, self.far[half]))
        self.pair = self.send(copies)

    def end(self):
        self.links.wait(self.pair, self.span(2))


LOAD_BUFFERS = ("mine", "give", "got", "first", "second_give", "second", "line_in", "out")


class Payload:
    def __init__(self, sz, b, links, index, output):
        self.sz, self.links, self.output = sz, links, output
        self.deep = sz.deeps[index]
        for name in LOAD_BUFFERS:
            setattr(self, name, getattr(b, "load_" + name)[index])
        half = lambda which: pl.ds(which * (sz.group // 2), sz.group // 2)
        self.plane = PlaneSum(
            links,
            lambda member, which: self.mine.at[member, half(which)],
            self.first,
            self.second_give,
            self.second,
        )
        self.spread = PlaneSpread(
            links,
            lambda member, which: self.got.at[member, half(which)],
            lambda count: self.got.at[pl.ds(0, count)],
        )
        self.half = half

    def matrix(self, place, values):
        sz = self.sz
        low = lax.axis_index("hid") == 0
        left = jnp.concatenate(values[: sz.side_blocks], axis=1)
        right = jnp.concatenate(values[sz.side_blocks :], axis=1)
        mine = jnp.where(low, left, right).astype(BF16)
        give = jnp.where(low, right, left).astype(BF16)
        count = sz.size // self.deep
        for part in range(count):
            index = place * count + part
            rows = slice(part * self.deep, (part + 1) * self.deep)
            self.mine[index // sz.group, index % sz.group] = mine[rows, :]
            self.give[index // sz.group, index % sz.group] = give[rows, :]

    def rows16(self, place, mine, give):
        index = place * (self.sz.size // self.deep)
        self.mine[index // self.sz.group, index % self.sz.group, 0:16] = mine.astype(BF16)
        self.give[index // self.sz.group, index % self.sz.group, 0:16] = give.astype(BF16)

    def to_partner(self):
        self.copy = self.links.sibling(self.give, self.got)

    def to_plane(self):
        done(self.copy)
        self.mine[...] = (self.mine[...].astype(F32) + self.got[...].astype(F32)).astype(BF16)
        self.plane.start()

    def middle(self):
        self.plane.middle()

    def to_line(self):
        self.plane.end()
        self.sums = self.plane.sums()
        links = self.links
        self.pair = links.in_line(self.sums, self.line_in.at[links.line])

    def back_line(self):
        links, sz = self.links, self.sz
        links.wait(self.pair, self.line_in.at[pl.ds(0, sz.group - 1)])
        self.line_in[links.line] = self.sums(links.line)[...]
        total = self.line_in[0].astype(F32)
        for member in range(1, sz.group):
            total += self.line_in[member].astype(F32)
        self.out[...] = total.astype(BF16)
        self.got[links.plane, links.line] = self.out[...]
        self.pair = links.in_line(lambda member: self.out, self.got.at[links.plane, links.line])

    def back_plane(self):
        self.links.wait(self.pair, self.got.at[0, pl.ds(0, self.sz.group - 1)])
        self.spread.start()

    def finish(self):
        self.spread.end()
        return self.links.load(self.got, self.output)


def greet_all(sz):
    me = lax.axis_index("rows") * sz.hid + lax.axis_index("hid")
    barrier = pltpu.get_barrier_semaphore()

    def greet(step, carry):
        peer = lax.rem(me + step, sz.count)
        pl.semaphore_signal(
            barrier,
            inc=1,
            device_id=(peer // sz.hid, lax.rem(peer, sz.hid)),
            device_id_type=MESH,
        )
        return carry

    lax.fori_loop(1, sz.count, greet, 0)
    return barrier


class Exchange:
    def __init__(self, sz, links):
        self.sz, self.links = sz, links
        self.odd = lax.rem(links.row, 2)
        self.token = links.row * sz.hid + links.col

    def channels(self, row, col, size):
        sz = self.sz
        start = col * sz.half + (row // 2) * sz.couple + lax.rem(row, 2) * sz.big
        return pl.ds(pl.multiple_of(start, 16), size)

    def block(self, token, size):
        return pl.ds(pl.multiple_of(token * self.sz.big, 16), size)

    def far_first(self):
        line = self.links.line
        odd = lax.rem(line, 2)
        across = 2 * (1 - line // 2)
        return across + odd, across + 1 - odd, line + 1 - 2 * odd, line

    def by_size(self, body):
        pl.when(self.odd == 0)(lambda: body(self.sz.big))
        pl.when(self.odd == 1)(lambda: body(self.sz.small))

    def local(self):
        local = self.links.local_sems.at[self.links.used_local]
        self.links.used_local += 1
        return local

    def to_owners(self, source, target):
        sz, links = self.sz, self.links
        pair, local = links.pair(), self.local()

        def own(size):
            pltpu.make_async_copy(
                source.at[self.channels(links.row, links.col, size)],
                target.at[self.block(self.token, size)],
                local,
            ).start()

        self.by_size(own)
        half = sz.peers * sz.hid // 2
        first = (links.plane // 2) * sz.hid + links.col

        for turn, line in enumerate(self.far_first()):

            def post(step, carry):
                index = lax.rem(first + step, half)
                col = lax.rem(index, sz.hid)
                for odd, size in ((0, sz.big), (1, sz.small)):
                    row = line * sz.peers + 2 * (index // sz.hid) + odd

                    def send():
                        links.copy(
                            source.at[self.channels(row, col, size)],
                            target.at[self.block(self.token, size)],
                            pair,
                            row,
                            col,
                        ).start()

                    if turn < sz.group - 1:
                        send()
                    else:
                        pl.when((step > 0) | (self.odd != odd))(send)
                return carry

            lax.fori_loop(0, half, post, 0)
        return pair, local

    def to_tokens(self, source, target):
        sz, links = self.sz, self.links
        pair, local = links.pair(), self.local()

        def send(size):
            mine = target.at[self.channels(links.row, links.col, size)]
            pltpu.make_async_copy(source.at[self.block(self.token, size)], mine, local).start()

            devices = sz.peers * sz.hid
            first = links.plane * sz.hid + links.col

            for turn, line in enumerate(self.far_first()):

                def post(step, carry):
                    index = lax.rem(first + step, devices)
                    row, col = line * sz.peers + index // sz.hid, lax.rem(index, sz.hid)
                    peer = row * sz.hid + col
                    links.copy(source.at[self.block(peer, size)], mine, pair, row, col).start()
                    return carry

                lax.fori_loop(0 if turn < sz.group - 1 else 1, devices, post, 0)

        self.by_size(send)
        return pair, local

    def wait(self, tokens, by_tokens, by_owners, sent_by_tokens):
        sz, links = self.sz, self.links
        pair, local = tokens

        def wait(size):
            first = by_owners.at[pl.ds(0, size)]
            pltpu.make_async_copy(first, first, local).wait()
            all_tokens = by_owners.at[pl.ds(0, (sz.count - 1) * size)]
            all_channels = by_tokens.at[pl.ds(0, sz.width - size)]
            sent, came = all_tokens, all_channels
            if sent_by_tokens:
                sent, came = came, sent
            links.copy(came, came, pair, links.row, 1 - links.col).wait_recv()
            links.copy(sent, sent, pair, links.row, 1 - links.col).wait_send()

        self.by_size(wait)

    def owners_wait(self, tokens, source, target):
        self.wait(tokens, source, target, True)

    def tokens_wait(self, tokens, source, target):
        self.wait(tokens, target, source, False)


CHUNK = 8


def place(index, size):
    return pl.ds(pl.multiple_of(index * size, size), size)


def dft(sz, b, source, base, stride, target, unroll=2):
    steps, outer = sz.steps, sz.outer

    def chunk(index, carry):
        cos = b.twist[:, :LANES]
        sin = b.twist[:, LANES:]
        for line in range(CHUNK):
            start = base + index * CHUNK + line
            b.wide[:, line * LANES : (line + 1) * LANES] = source[
                pl.ds(start, steps, stride=stride), :
            ].astype(BF16)
        b.mid[...] = nn(b.outer_fwd[...], b.wide[...])
        for line in range(CHUNK):
            lanes = slice(line * LANES, (line + 1) * LANES)
            real = b.mid[0:outer, lanes]
            imag = b.mid[outer : 2 * outer, lanes]
            rows = slice(line * outer, (line + 1) * outer)
            b.turned[rows, 0:LANES] = (real * cos + imag * sin).astype(BF16)
            b.turned[rows, LANES:] = (imag * cos - real * sin).astype(BF16)
        target[place(index, CHUNK * outer), :] = nn(b.turned[...], b.inner_fwd[...])
        return carry

    lax.fori_loop(0, sz.big // CHUNK, chunk, 0, unroll=unroll)


def inverse_dft(sz, b, target, base, stride, unroll=2):
    steps, outer = sz.steps, sz.outer

    def chunk(index, carry):
        cos = b.twist[:, :LANES]
        sin = b.twist[:, LANES:]
        part = nn(b.flat[place(index, CHUNK * outer), :], b.inner_inv[...])
        for line in range(CHUNK):
            rows = slice(line * outer, (line + 1) * outer)
            lanes = slice(line * LANES, (line + 1) * LANES)
            real = part[rows, :LANES]
            imag = part[rows, LANES:]
            b.mid_half[0:outer, lanes] = (real * cos - imag * sin).astype(BF16)
            b.mid_half[outer : 2 * outer, lanes] = (imag * cos + real * sin).astype(BF16)
        value = nn(b.outer_inv[...], b.mid_half[...])
        for line in range(CHUNK):
            start = base + index * CHUNK + line
            target[pl.ds(start, steps, stride=stride), :] = value[
                :, line * LANES : (line + 1) * LANES
            ]
        return carry

    lax.fori_loop(0, sz.big // CHUNK, chunk, 0, unroll=unroll)


def first_channel(sz):
    row = lax.axis_index("rows")
    return (row // 2) * sz.couple + lax.rem(row, 2) * sz.big


def own_taps(sz, filters):
    start = first_channel(sz)
    chan = lax.broadcasted_iota(jnp.int32, (sz.big, sz.half), 0)
    lane = lax.broadcasted_iota(jnp.int32, (sz.big, sz.half), 1)
    pick = jnp.where(lane == start + chan, 1.0, 0.0).astype(BF16)
    parts = [nt(pick, filters[way].astype(BF16)) for way in range(2)]
    return jnp.concatenate(parts, axis=0).astype(BF16)


def own_envelope(sz, env):
    first_chan = lax.axis_index("hid") * sz.half + first_channel(sz)
    channel = first_chan + lax.broadcasted_iota(jnp.int32, (sz.big, LANES), 0)
    fraction = lax.rem(channel * 37, sz.width).astype(F32) / (sz.width - 1)
    start_log = math.log(1.0 / 40.0)
    rate = jnp.exp(start_log + (math.log(1.5 / sz.length) - start_log) * fraction)
    lane = lax.broadcasted_iota(jnp.int32, (sz.big, LANES), 1)

    def decays(step, power):
        decay = jnp.exp(-(lane + step * LANES).astype(F32) * rate)
        env[0 : sz.big, place(step, LANES)] = decay
        return power + decay * decay

    power = lax.fori_loop(0, sz.steps, decays, jnp.zeros((sz.big, LANES), F32), unroll=4)
    scale = lax.rsqrt(2.0 * jnp.sum(power, axis=1, keepdims=True))

    def scaled(step, carry):
        value = env[0 : sz.big, place(step, LANES)] * scale
        env[0 : sz.big, place(step, LANES)] = value
        env[sz.big :, place(step, LANES)] = jnp.where(lane + step * LANES > 0, value, 0.0)
        return carry

    lax.fori_loop(0, sz.steps, scaled, 0, unroll=4)


def filter_spectrum(sz, b, layer):
    piece, steps, outer = sz.big, sz.steps, sz.outer
    taps = own_taps(sz, b.filters[layer])
    count = 4

    def chunk(index, carry):
        lanes = place(index, count * LANES)
        kernels = nn(taps, b.pos[:, lanes]) * b.env[:, lanes]
        rows = pl.multiple_of(index * count * 2 * piece, 2 * piece)
        for step in range(count):
            b.tall[pl.ds(rows + step * 2 * piece, 2 * piece), :] = kernels[
                :, step * LANES : (step + 1) * LANES
            ]
        return carry

    lax.fori_loop(0, steps // count, chunk, 0, unroll=2)
    spec = b.filt_spec[layer]
    span = sz.big * outer
    for way in range(2):
        dft(sz, b, b.tall, way * piece, 2 * piece, b.spec)
        if way == 0:
            spec[...] = b.spec[0:span, :].astype(BF16)
        else:
            spec[:, :LANES] = (spec[:, :LANES].astype(F32) + b.spec[0:span, :LANES]).astype(BF16)
            spec[:, LANES:] = (spec[:, LANES:].astype(F32) - b.spec[0:span, LANES:]).astype(BF16)


def conv_forward(sz, b, layer, landed):
    b.tall[0 : sz.count * sz.big, :] = landed[...].astype(F32)
    dft(sz, b, b.tall, 0, sz.big, b.spec, True)
    span = sz.big * sz.outer
    filt = b.filt_spec[layer]
    for seq in range(sz.seqs):
        rows = slice(seq * span, (seq + 1) * span)
        re, im = b.spec[rows, :LANES], b.spec[rows, LANES:]
        b.sig_spec[layer][rows, :LANES] = re.astype(BF16)
        b.sig_spec[layer][rows, LANES:] = im.astype(BF16)
        fil_re, fil_im = filt[:, :LANES].astype(F32), filt[:, LANES:].astype(F32)
        b.flat[rows, :LANES] = (re * fil_re - im * fil_im).astype(BF16)
        b.flat[rows, LANES:] = (re * fil_im + im * fil_re).astype(BF16)
    inverse_dft(sz, b, b.tall, 0, sz.big, True)
    b.staged[...] = b.tall[0 : sz.count * sz.big, :].astype(BF16)


def conv_backward(sz, b, layer, landed):
    b.tall[0 : sz.count * sz.big, :] = landed[...].astype(F32)
    dft(sz, b, b.tall, 0, sz.big, b.spec, True)
    span = sz.big * sz.outer
    filt = b.filt_spec[layer]
    for seq in range(sz.seqs):
        rows = slice(seq * span, (seq + 1) * span)
        re, im = b.spec[rows, :LANES], b.spec[rows, LANES:]
        fil_re, fil_im = filt[:, :LANES].astype(F32), filt[:, LANES:].astype(F32)
        b.flat[rows, :LANES] = (re * fil_re + im * fil_im).astype(BF16)
        b.flat[rows, LANES:] = (im * fil_re - re * fil_im).astype(BF16)
    inverse_dft(sz, b, b.tall, 0, sz.big, True)
    b.staged[...] = b.tall[0 : sz.count * sz.big, :].astype(BF16)


def taps_gradient(sz, b, layer, landed, signal):
    span = sz.big * sz.outer
    total_re = jnp.zeros((span, LANES), F32)
    total_im = jnp.zeros((span, LANES), F32)
    for seq in range(sz.seqs):
        rows = slice(seq * span, (seq + 1) * span)
        re, im = b.spec[rows, :LANES], b.spec[rows, LANES:]
        sig = b.sig_spec[layer]
        sig_re, sig_im = sig[rows, :LANES].astype(F32), sig[rows, LANES:].astype(F32)
        total_re += re * sig_re + im * sig_im
        total_im += im * sig_re - re * sig_im
    piece = sz.big
    b.tall[...] = jnp.zeros_like(b.tall)
    for way in range(2):
        b.flat[0:span, :LANES] = total_re.astype(BF16)
        b.flat[0:span, LANES:] = (total_im if way == 0 else -total_im).astype(BF16)
        inverse_dft(sz, b, b.tall, way * piece, 2 * piece)
    taps = own_taps(sz, b.filters[layer])
    count = 4

    def chunk(index, total):
        lanes = place(index, count * LANES)
        rows = pl.multiple_of(index * count * 2 * piece, 2 * piece)
        raw = nn(taps, b.pos[:, lanes])
        grads = jnp.concatenate(
            [b.tall[pl.ds(rows + step * 2 * piece, 2 * piece), :] for step in range(count)],
            axis=1,
        )
        grads = grads * b.env[:, lanes] + (2.0 * DECAY) * raw
        return total + nt(grads.astype(BF16), b.pos[:, lanes])

    start = jnp.zeros((2 * piece, ORDER), F32)
    total = lax.fori_loop(0, sz.steps // count, chunk, start, unroll=2)

    def product(block, products):
        rows = place(block, piece)
        return products + landed[rows, :].astype(F32) * signal[rows, :].astype(F32)

    start = jnp.zeros((piece, LANES), F32)
    products = lax.fori_loop(0, sz.count, product, start, unroll=8)
    column = jnp.sum(products, axis=1, keepdims=True)
    row = jnp.transpose(jnp.broadcast_to(column, (piece, LANES)))[0:8, :]
    b.taps_work[...] = jnp.zeros_like(b.taps_work)
    b.taps_work[0 : sz.big, :] = total[0 : sz.big, :]
    b.taps_work[sz.big : 2 * sz.big, :] = total[piece : piece + sz.big, :]
    b.taps_work[2 * sz.big : 2 * sz.big + 1, 0:piece] = row[0:1, :]


def block_of(sz, block):
    return slice(block * sz.size, (block + 1) * sz.size)


def project(sz, b, layer):
    for block in range(sz.blocks):
        rows = block_of(sz, block)
        part = b.normed[layer][:, rows]
        b.inner[layer][rows, :] = nt(b.mixer[layer, 0, block], part).astype(BF16)
        b.gate[layer][rows, :] = nt(b.mixer[layer, 1, block], part)


def mix(sz, b, layer, conv):
    summed, mixed, middle = b.summed[layer], b.mixed[layer], b.middle[layer]
    summed[...] = conv[...].astype(F32) + b.skip[layer][...] * b.inner[layer][...].astype(F32)
    mixed[...] = (b.gate[layer][...] * summed[...]).astype(BF16)
    for block in range(sz.blocks):
        rows = block_of(sz, block)
        middle[:, rows] = tn(mixed[rows, :], b.mixer[layer, 2, block])
    middle[...] = middle[...] + b.stream[layer][...]


def mixer_gradient(sz, b, kind_row, values, mine, give):
    low = lax.axis_index("hid") == 0
    left = jnp.concatenate(values[: sz.side_blocks], axis=1)
    right = jnp.concatenate(values[sz.side_blocks :], axis=1)
    rows = slice(kind_row * sz.size, (kind_row + 1) * sz.size)
    mine[rows, :] = jnp.where(low, left, right).astype(BF16)
    give[rows, :] = jnp.where(low, right, left).astype(BF16)


def gain_gradient(sz, b, row, value, mine, give):
    low = lax.axis_index("hid") == 0
    left, right = value[:, : sz.half], value[:, sz.half :]
    mine[row : row + 1, :] = jnp.where(low, left, right)
    give[row : row + 1, :] = jnp.where(low, right, left)


def mixer_backward(sz, b, layer, grad_next, total):
    normal, inv = normalize(b.middle[layer][...])
    gain = b.gain[layer, 1:2, :]
    back, gain_grad = norm_back(total, normal, inv, gain)
    result = grad_next + back
    b.grad_middle[...] = result
    b.grad_o[...] = result.astype(BF16)
    for block in range(sz.blocks):
        rows = block_of(sz, block)
        grad_mixed = nt(b.mixer[layer, 2, block], b.grad_o[:, rows])
        b.gate_grad[rows, :] = (grad_mixed * b.summed[layer][rows, :]).astype(BF16)
        through = grad_mixed * b.gate[layer][rows, :]
        b.summed_grad[rows, :] = through
        b.conv_grad[rows, :] = through.astype(BF16)
    return gain_grad


def out_gradient(sz, b, layer):
    return [
        nn(b.mixed[layer][block_of(sz, block), :], b.grad_o[:, block_of(sz, block)])
        for block in range(sz.blocks)
    ]


def in_gradient(sz, b, layer, grads):
    return [
        jnp.transpose(
            nn(grads[block_of(sz, block), :], b.normed[layer][:, block_of(sz, block)])
        )
        for block in range(sz.blocks)
    ]


def input_backward(sz, b, layer, back):
    direct = b.skip[layer][...] * b.summed_grad[...]
    b.inner_grad[...] = (direct + back[...].astype(F32)).astype(BF16)
    for block in range(sz.blocks):
        rows = block_of(sz, block)
        b.grad_sum[0 : sz.own, rows] = tn(b.inner_grad[rows, :], b.mixer[layer, 0, block]) + tn(
            b.gate_grad[rows, :], b.mixer[layer, 1, block]
        )
    normal, inv = normalize(b.stream[layer][...])
    result, gain_grad = norm_back(
        b.grad_sum[0 : sz.own, :], normal, inv, b.gain[layer, 0:1, :]
    )
    return b.grad_middle[...] + result, gain_grad


def ff_forward(sz, b, layer):
    tile = 512
    rows = slice(0, 2 * sz.own)
    b.out_sum[...] = jnp.zeros_like(b.out_sum)

    def body(step, carry):
        lanes = pl.ds(pl.multiple_of(step * tile, tile), tile)
        normed = b.nbuf[layer][rows, :]
        gate = nn(normed, b.up[layer, 0, :, lanes])
        up = nn(normed, b.up[layer, 1, :, lanes])
        value, _ = gelu_parts(gate)
        b.out_sum[...] += nt((value * up).astype(BF16), b.down[layer, :, lanes])
        return carry

    lax.fori_loop(0, sz.units // tile, body, 0)


def ff_backward(sz, b, layer, with_out):
    tile = 512
    rows = slice(0, 2 * sz.own)
    b.grad_sum[...] = jnp.zeros_like(b.grad_sum)
    if with_out:
        b.out_sum[...] = jnp.zeros_like(b.out_sum)

    def body(step, carry):
        lanes = pl.ds(pl.multiple_of(step * tile, tile), tile)
        normed = b.nbuf[layer][rows, :]
        gate = nn(normed, b.up[layer, 0, :, lanes])
        up = nn(normed, b.up[layer, 1, :, lanes])
        through = nn(b.gbuf[layer][rows, :], b.down[layer, :, lanes])
        value, slope = gelu_parts(gate)
        if with_out:
            b.out_sum[...] += nt((value * up).astype(BF16), b.down[layer, :, lanes])
        gate_grad = (slope * up * through).astype(BF16)
        up_grad = (value * through).astype(BF16)
        b.grad_sum[...] += nt(gate_grad, b.up[layer, 0, :, lanes]) + nt(
            up_grad, b.up[layer, 1, :, lanes]
        )
        return carry

    lax.fori_loop(0, sz.units // tile, body, 0)


def ff_gradients(sz, b, layer, links, between=(None, None, None)):
    start = pl.multiple_of(links.line * sz.part, LANES)
    units = pl.ds(start, sz.part)
    chunk = 2 * sz.own

    def body(step, carry):
        rows = pl.ds(pl.multiple_of(step * chunk, chunk), chunk)
        normed = b.nbuf[layer][rows, :]
        gate = nn(normed, b.up[layer, 0, :, units])
        up = nn(normed, b.up[layer, 1, :, units])
        through = nn(b.gbuf[layer][rows, :], b.down[layer, :, units])
        value, slope = gelu_parts(gate)
        b.unit_grad[0, rows, :] = (slope * up * through).astype(BF16)
        b.unit_grad[1, rows, :] = (value * through).astype(BF16)
        b.unit_grad[2, rows, :] = (value * up).astype(BF16)
        return carry

    lax.fori_loop(0, sz.group, body, 0)
    split = sz.width // 2
    moving = []
    for kind in range(3):
        if between[kind] is not None:
            between[kind]()
        left = b.gbuf[layer] if kind == 2 else b.nbuf[layer]

        def part(index, carry):
            lanes = place(index, split)
            b.product[...] = tn(left[:, lanes], b.unit_grad[kind])
            count = split // sz.depth
            for each in range(count):
                line = index * (count // sz.peers) + each // sz.peers
                rows = slice(each * sz.depth, (each + 1) * sz.depth)
                b.pieces[kind, each % sz.peers, line, 0 : sz.depth, :] = b.product[rows, :].astype(
                    BF16
                )
            return carry

        lax.fori_loop(0, 2, part, 0)
        half = lambda which: pl.ds(which * (sz.group // 2), sz.group // 2)
        plane = PlaneSum(
            links,
            lambda member, which, kind=kind: b.pieces.at[kind, member, half(which)],
            b.plane_first[layer].at[kind],
            b.plane_give[layer].at[kind],
            b.plane_second[layer].at[kind],
        )
        plane.start()
        moving.append(plane)
    return moving


def done(copy):
    copy.wait()


class Named:
    pass


def layout(sz):
    layers, own, width = sz.layers, sz.own, sz.width
    wide = 2 * sz.big * sz.steps
    late = sz.late_rows * sz.rows
    per_layer = dict(
        stream=((own, width), F32),
        normed=((own, width), BF16),
        inner=((width, own), BF16),
        gate=((width, own), F32),
        summed=((width, own), F32),
        mixed=((width, own), BF16),
        middle=((own, width), F32),
        nbuf=((2 * sz.group * own, width), BF16),
        gbuf=((2 * sz.group * own, width), BF16),
        skip=((width, LANES), F32),
        filt_spec=((sz.big * sz.outer, 2 * LANES), BF16),
        sig_spec=((sz.pairs * sz.outer, 2 * LANES), BF16),
        fore_in=((sz.count * sz.big, LANES), BF16),
        fore_out=((width, own), BF16),
        back_in=((sz.count * sz.big, LANES), BF16),
        back_out=((width, own), BF16),
        plane_first=((3, 2, 2, sz.group // 2, sz.deep, sz.part), BF16),
        plane_give=((3, 2, sz.group // 2, sz.deep, sz.part), BF16),
        plane_second=((3, 2, sz.group // 2, sz.deep, sz.part), BF16),
        grad_got=((own, width), BF16),
        out_got=((own, width), BF16),
    )
    single = dict(
        x=((own, width), BF16),
        gain=((layers, 2, width), F32),
        skip_rows=((layers, width), F32),
        mixer=((layers, 3, sz.blocks, sz.size, sz.size), BF16),
        filters=((layers, 2, ORDER, sz.half), F32),
        pos=((ORDER, sz.length), BF16),
        outer_fwd=((2 * sz.outer, sz.steps), BF16),
        outer_inv=((sz.steps, 2 * sz.outer), BF16),
        inner_fwd=((2 * LANES, 2 * LANES), BF16),
        inner_inv=((2 * LANES, 2 * LANES), BF16),
        twist=((sz.outer, 2 * LANES), F32),
        up=((layers, 2, width, sz.units), BF16),
        down=((layers, width, sz.units), BF16),
        env=((2 * sz.big, sz.length), F32),
        tall=((max(wide, sz.count * sz.big), LANES), F32),
        wide=((sz.steps, CHUNK * LANES), BF16),
        turned=((CHUNK * sz.outer, 2 * LANES), BF16),
        mid=((2 * sz.outer, CHUNK * LANES), F32),
        flat=((sz.pairs * sz.outer, 2 * LANES), BF16),
        mid_half=((2 * sz.outer, CHUNK * LANES), BF16),
        spec=((sz.pairs * sz.outer, 2 * LANES), F32),
        conv_grad=((width, own), BF16),
        staged=((sz.count * sz.big, LANES), BF16),
        grad_middle=((own, width), F32),
        grad_o=((own, width), BF16),
        gate_grad=((width, own), BF16),
        summed_grad=((width, own), F32),
        inner_grad=((width, own), BF16),
        out_sum=((2 * own, width), F32),
        grad_sum=((2 * own, width), F32),
        out_give=((own, width), BF16),
        sum_give=((own, width), BF16),
        unit_grad=((3, 2 * sz.group * own, sz.part), BF16),
        product=((width // 2, sz.part), F32),
        pieces=((3, sz.peers, sz.group, sz.deep, sz.part), BF16),
        taps_work=((sz.taps_rows, ORDER), F32),
        gain_mine=((16, sz.half), F32),
        gain_give=((16, sz.half), F32),
        late_gain_mine=((16, sz.half), F32),
        late_gain_give=((16, sz.half), F32),
        late_mine=((late, sz.half), BF16),
        late_give=((late, sz.half), BF16),
        late_got=((late, sz.half), BF16),
        late_in=((sz.rows, sz.late_rows, sz.half), BF16),
        late_sum=((sz.late_rows, sz.half), BF16),
        out_keep=((2, own, sz.half), BF16),
        taps_line=((layers, sz.group, sz.taps_rows, ORDER), BF16),
        late_out=((sz.late_rows, sz.half), BF16),
    )
    names, specs = [], []
    for name, (shape, kind) in per_layer.items():
        for layer in range(layers):
            names.append((name, layer))
            specs.append(pltpu.VMEM(shape, kind))
    for index, deep in enumerate(sz.deeps):
        part = (sz.group // 2, deep, sz.half)
        whole_load = (sz.peers, sz.group, deep, sz.half)
        line = (sz.group, deep, sz.half)
        shapes = (whole_load,) * 3 + ((2, 2) + part, (2,) + part, (2,) + part, line, line[1:])
        for name, shape in zip(LOAD_BUFFERS, shapes):
            names.append(("load_" + name, index))
            specs.append(pltpu.VMEM(shape, BF16))
    for name, (shape, kind) in single.items():
        names.append((name, None))
        specs.append(pltpu.VMEM(shape, kind))
    return names, specs


TABLES = ("pos", "outer_fwd", "outer_inv", "inner_fwd", "inner_inv", "twist")
INPUTS = ("hidden_in", "d_out", "gains", "mixer", "skip", "filters", "gate_up", "down") + TABLES
OUTPUTS = ("hidden_out", "grad_in", "upper", "lower", "late", "taps", "units")


def program_kernel(sz, *refs):
    names, _ = layout(sz)
    inputs = dict(zip(INPUTS, refs))
    outputs = dict(zip(OUTPUTS, refs[len(INPUTS) :]))
    scratch = refs[len(INPUTS) + len(OUTPUTS) :]
    b = Named()
    for (name, layer), ref in zip(names, scratch):
        if layer is None:
            setattr(b, name, ref)
        else:
            setattr(b, name, getattr(b, name, ()) + (ref,))
    links = Links(sz, scratch[len(names)], scratch[len(names) + 1])
    own = sz.own
    top = sz.layers - 1
    col = links.col
    low = col == 0
    mine_rows = pl.ds(pl.multiple_of(col * own, own), own)
    other_rows = pl.ds(pl.multiple_of((1 - col) * own, own), own)

    barrier = greet_all(sz)
    lanes = pl.ds(pl.multiple_of(col * sz.half, sz.half), sz.half)
    sides = pl.ds(col * sz.side_blocks, sz.side_blocks)
    slots = lambda first, count: pl.ds(first * own, count * own)
    near_slots, line_slots, far_slots = slots(0, 2), slots(2, 3), slots(5, 3)
    halves = {
        "x": (inputs["hidden_in"].at[mine_rows], b.x.at[:, lanes]),
        "gains": (inputs["gains"], b.gain.at[:, :, lanes]),
        "mixer": (inputs["mixer"].at[0, pl.ds(0, 2)], b.mixer.at[0, pl.ds(0, 2), sides]),
        "skip": (inputs["skip"], b.skip_rows.at[:, lanes]),
        "out_mixer": (inputs["mixer"].at[0, pl.ds(2, 1)], b.mixer.at[0, pl.ds(2, 1), sides]),
    }
    if sz.layers > 1:
        above = pl.ds(1, sz.layers - 1)
        halves["mixers"] = (inputs["mixer"].at[above], b.mixer.at[above, :, sides])
    loads = {name: links.load(*pair) for name, pair in halves.items()}
    for name in ("filters",) + TABLES:
        loads[name] = links.load(inputs[name], getattr(b, name))
    grads = b.gbuf[top]
    loads["g"] = links.load(inputs["d_out"].at[mine_rows], grads.at[slots(0, 1), lanes])
    loads["g_near"] = links.load(inputs["d_out"].at[other_rows], grads.at[slots(1, 1), lanes])
    b.gain_mine[...] = jnp.zeros_like(b.gain_mine)
    b.gain_give[...] = jnp.zeros_like(b.gain_give)
    b.late_gain_mine[...] = jnp.zeros_like(b.late_gain_mine)
    b.late_gain_give[...] = jnp.zeros_like(b.late_gain_give)
    pl.semaphore_wait(barrier, sz.count - 1)
    got = {}
    for name, (source, target) in halves.items():
        if name == "x":
            source = inputs["hidden_in"].at[other_rows]
        got[name] = links.sibling(source, target)
    got["g"] = links.sibling(inputs["d_out"].at[other_rows], grads.at[slots(0, 1), lanes])
    got["g_near"] = links.sibling(inputs["d_out"].at[mine_rows], grads.at[slots(1, 1), lanes])

    def both(*wanted):
        for name in wanted:
            done(loads[name])
            done(got[name])

    def turn_mixer(layer, kind):
        for block in range(sz.blocks):
            b.mixer[layer, kind, block] = jnp.transpose(b.mixer[layer, kind, block])

    def norm_to(source, target, layer, which):
        normal, _ = normalize(source)
        target[...] = (normal * b.gain[layer, which : which + 1, :]).astype(BF16)

    def slot_of(place, member):
        return 2 + (member if member < place else member - 1)

    class Gather:
        moves = (
            {0: [(0, 1)], 1: [(1, 0), (1, 2)], 2: [(2, 1), (2, 3)], 3: [(3, 2)]},
            {1: [(2, 0), (0, 2)], 2: [(3, 1), (1, 3)]},
            {1: [(3, 0)], 2: [(0, 3)]},
        )
        coming = ((1, 2, 2, 1), (1, 1, 1, 1), (1, 0, 0, 1))

        def __init__(self, buffer):
            self.buffer = buffer
            self.pairs = [None] * 3

        def near(self):
            return links.sibling(self.buffer.at[slots(0, 1)], self.buffer.at[slots(1, 1)])

        def views(self, place, whose, target):
            here = 0 if whose == place else slot_of(place, whose)
            there = slot_of(target, whose)
            return [(self.buffer.at[slots(here, 1)], self.buffer.at[slots(there, 1)])]

        def span(self, count):
            return self.buffer.at[slots(0, count)]

        def step(self, index):
            if index > 0:
                self.wait(index - 1)
            pair = links.pair()
            for place, moves in self.moves[index].items():

                @pl.when(links.line == place)
                def _():
                    for whose, target in moves:
                        for source, there in self.views(place, whose, target):
                            row = target * sz.peers + links.plane
                            links.copy(source, there, pair, row, col).start()

            self.pairs[index] = pair

        def wait(self, index):
            pair = self.pairs[index]
            if True:
                for place in range(sz.group):
                    came = self.coming[index][place]
                    sent = len(self.moves[index].get(place, ()))

                    @pl.when(links.line == place)
                    def _():
                        if came:
                            span = self.span(came)
                            links.copy(span, span, pair, links.row, 1 - col).wait_recv()
                        if sent:
                            span = self.span(sent)
                            links.copy(span, span, pair, links.row, 1 - col).wait_send()

        def rest(self):
            self.wait(2)
            self.copies = [links.sibling(self.buffer.at[line_slots], self.buffer.at[far_slots])]

        def finish(self):
            for copy in self.copies:
                done(copy)

    class ArgumentGather(Gather):
        def views(self, place, whose, target):
            there = slot_of(target, whose)
            pairs = []
            for rows, shift in ((mine_rows, 0), (other_rows, 3)):
                if whose == place:
                    source = inputs["d_out"].at[rows]
                else:
                    source = self.buffer.at[slots(slot_of(place, whose) + shift, 1), lanes]
                pairs.append((source, self.buffer.at[slots(there + shift, 1), lanes]))
            return pairs

        def span(self, count):
            return self.buffer.at[slots(0, 2 * count), lanes]

        def rest(self):
            self.wait(2)
            self.copies = [
                links.sibling(self.buffer.at[line_slots, lanes], self.buffer.at[far_slots, lanes]),
                links.sibling(self.buffer.at[far_slots, lanes], self.buffer.at[line_slots, lanes]),
            ]

    top_grads = ArgumentGather(grads)
    top_grads.step(0)
    both("x", "gains")
    b.stream[0][...] = b.x[...].astype(F32)
    norm_to(b.stream[0][...], b.normed[0], 0, 0)
    both("mixer")
    turn_mixer(0, 0)
    turn_mixer(0, 1)

    exchange = Exchange(sz, links)
    project(sz, b, 0)
    normed_parts = []
    for layer in range(sz.layers):
        moving = exchange.to_owners(b.inner[layer], b.fore_in[layer])
        if layer == 0:
            for each in range(sz.layers):
                loads["up", each] = links.load(inputs["gate_up"].at[each], b.up.at[each])
                loads["down", each] = links.load(inputs["down"].at[each], b.down.at[each])
            for name in ("filters", "pos", "outer_fwd", "inner_fwd", "twist"):
                done(loads[name])
            own_envelope(sz, b.env)
            filter_spectrum(sz, b, 0)
            for name in ("outer_inv", "inner_inv"):
                done(loads[name])
            both("skip", "g", "g_near")
            for each in range(sz.layers):
                row = b.skip_rows[each : each + 1, :]
                b.skip[each][...] = jnp.transpose(jnp.broadcast_to(row, (LANES, sz.width)))
        exchange.owners_wait(moving, b.inner[layer], b.fore_in[layer])
        if layer == 0:
            top_grads.step(1)
        else:
            top_grads.rest()
        conv_forward(sz, b, layer, b.fore_in[layer])
        moving = exchange.to_tokens(b.staged, b.fore_out[layer])
        if layer == 0:
            both("out_mixer")
            if sz.layers > 1:
                both("mixers")
            for each in range(1, sz.layers):
                turn_mixer(each, 0)
                turn_mixer(each, 1)
        if layer < top:
            filter_spectrum(sz, b, layer + 1)
        done(loads["up", layer])
        done(loads["down", layer])
        if layer == 0:
            top_grads.step(2)
        exchange.tokens_wait(moving, b.staged, b.fore_out[layer])
        mix(sz, b, layer, b.fore_out[layer])
        norm_to(b.middle[layer][...], b.nbuf[layer].at[slots(0, 1)], layer, 1)
        normed_parts.append(Gather(b.nbuf[layer]))
        near = normed_parts[layer].near()
        if layer == top:
            normed_parts[layer].step(0)
        done(near)
        if layer < top:
            ff_forward(sz, b, layer)
            b.out_give[...] = b.out_sum[own:, :].astype(BF16)
            moving = links.sibling(b.out_give, b.out_got[layer])
            done(moving)
            value = b.middle[layer][...] + b.out_sum[0:own, :] + b.out_got[layer][...].astype(F32)
            b.stream[layer + 1][...] = value
            norm_to(value, b.normed[layer + 1], layer + 1, 0)
            project(sz, b, layer + 1)

    ff_backward(sz, b, top, True)
    b.sum_give[...] = b.grad_sum[own:, :].astype(BF16)
    moving = links.sibling(b.sum_give, b.grad_got[top])
    b.out_give[...] = b.out_sum[own:, :].astype(BF16)
    out_moving = links.sibling(b.out_give, b.out_got[top])
    normed_parts[top].step(1)
    done(moving)
    total = b.grad_sum[0:own, :] + b.grad_got[top][...].astype(F32)
    grad_next = b.gbuf[top][0:own, :].astype(F32)
    gain_grad = mixer_backward(sz, b, top, grad_next, total)
    moving = exchange.to_owners(b.conv_grad, b.back_in[top])
    gain_gradient(sz, b, 2 * top, gain_grad, b.gain_mine, b.gain_give)
    upper = Payload(sz, b, links, 0, outputs["upper"])
    lower = Payload(sz, b, links, 1, outputs["lower"])
    upper.matrix(0, out_gradient(sz, b, top))
    done(out_moving)
    value = b.middle[top][...] + b.out_sum[0:own, :] + b.out_got[top][...].astype(F32)
    value = value.astype(BF16)
    left, right = value[:, : sz.half], value[:, sz.half :]
    b.out_keep[0] = jnp.where(low, left, right)
    b.out_keep[1] = jnp.where(low, right, left)
    place = outputs["hidden_out"].at[mine_rows]
    ending = [links.load(b.out_keep.at[0], place), links.sibling(b.out_keep.at[1], place)]
    top_grads.finish()
    normed_parts[top].step(2)

    plane_moving = {}
    taps_moving = {}
    units_moving = []

    def taps_to_line(layer):
        taps_gradient(sz, b, layer, b.back_in[layer], b.fore_in[layer])
        place = b.taps_line.at[layer, links.line]
        b.taps_line[layer, links.line] = b.taps_work[...].astype(BF16)
        taps_moving[layer] = links.in_line(lambda member: place, place)

    def taps_to_plane(layer):
        links.wait(taps_moving[layer], b.taps_line.at[layer, pl.ds(0, sz.group - 1)])
        place = outputs["taps"].at[layer, links.plane]
        ending.append(links.load(b.taps_line.at[layer], place))
        taps_moving[layer] = links.in_plane(lambda member: b.taps_line.at[layer], place)

    def units_middle(layer, kinds=(0, 1, 2)):
        for kind in kinds:
            plane_moving[layer][kind].middle()

    def units_end(layer, kinds=(0, 1, 2)):
        for kind in kinds:
            plane = plane_moving[layer][kind]
            plane.end()
            part = plane.sums()
            target = outputs["units"].at[layer, kind, links.line]
            ending.append(links.load(part(links.line), target))
            pair = links.in_line(part, target)
            units_moving.append((layer, kind, pair))

    exchange.owners_wait(moving, b.conv_grad, b.back_in[top])
    conv_backward(sz, b, top, b.back_in[top])
    moving = exchange.to_tokens(b.staged, b.back_out[top])
    normed_parts[top].rest()
    normed_parts[0].step(0)
    normed_parts[top].finish()
    plane_moving[top] = ff_gradients(sz, b, top, links)
    exchange.tokens_wait(moving, b.staged, b.back_out[top])
    value, gain_grad = input_backward(sz, b, top, b.back_out[top])
    b.out_sum[0:own, :] = value
    b.gbuf[0][0:own, :] = value.astype(BF16)
    gather = Gather(b.gbuf[0])
    near = gather.near()
    gather.step(0)
    normed_parts[0].step(1)
    gain_gradient(sz, b, 2 * top - 1, gain_grad, b.gain_mine, b.gain_give)
    upper.matrix(1, in_gradient(sz, b, top, b.inner_grad))
    upper.matrix(2, in_gradient(sz, b, top, b.gate_grad))
    upper.to_partner()
    done(near)
    ff_backward(sz, b, 0, False)
    b.sum_give[...] = b.grad_sum[own:, :].astype(BF16)
    moving = links.sibling(b.sum_give, b.grad_got[0])
    gather.step(1)
    normed_parts[0].step(2)
    done(moving)
    total = b.grad_sum[0:own, :] + b.grad_got[0][...].astype(F32)
    gain_grad = mixer_backward(sz, b, 0, b.out_sum[0:own, :], total)

    moving = exchange.to_owners(b.conv_grad, b.back_in[0])
    units_middle(top)
    upper.to_plane()
    taps_to_line(top)
    gain_gradient(sz, b, 0, gain_grad, b.gain_mine, b.gain_give)
    lower.matrix(0, out_gradient(sz, b, 0))
    lower.matrix(1, in_gradient(sz, b, 0, b.gate_grad))
    lower.rows16(2, b.gain_mine[...], b.gain_give[...])
    lower.to_partner()
    gather.step(2)
    exchange.owners_wait(moving, b.conv_grad, b.back_in[0])
    lower.to_plane()
    conv_backward(sz, b, 0, b.back_in[0])
    moving = exchange.to_tokens(b.staged, b.back_out[0])
    units_end(top)
    normed_parts[0].rest()
    gather.rest()
    upper.middle()
    taps_to_plane(top)
    normed_parts[0].finish()
    gather.finish()
    between = (lower.middle, upper.to_line, None)
    plane_moving[0] = ff_gradients(sz, b, 0, links, between)
    exchange.tokens_wait(moving, b.staged, b.back_out[0])
    value, gain_grad = input_backward(sz, b, 0, b.back_out[0])

    left, right = value[:, : sz.half], value[:, sz.half :]
    keep, give = b.out_sum.at[0:own, 0 : sz.half], b.out_sum.at[own:, 0 : sz.half]
    keep[...] = jnp.where(low, left, right)
    give[...] = jnp.where(low, right, left)
    mixer_gradient(sz, b, 0, in_gradient(sz, b, 0, b.inner_grad), b.late_mine, b.late_give)
    gain_gradient(sz, b, 0, gain_grad, b.late_gain_mine, b.late_gain_give)
    rows = slice(sz.size, sz.size + 16)
    b.late_mine[rows, :] = b.late_gain_mine[...].astype(BF16)
    b.late_give[rows, :] = b.late_gain_give[...].astype(BF16)
    last = slice(sz.size + 16, sz.rows * sz.late_rows)
    b.late_mine[last, :] = jnp.zeros_like(b.late_mine[last, :])
    b.late_give[last, :] = jnp.zeros_like(b.late_give[last, :])
    late_pair = links.sibling(b.late_give, b.late_got)
    place = outputs["grad_in"].at[mine_rows]
    ending += [links.load(keep, place), links.sibling(give, place)]

    done(late_pair)
    b.late_mine[...] = (b.late_mine[...].astype(F32) + b.late_got[...].astype(F32)).astype(BF16)
    few = lambda index: pl.ds(pl.multiple_of(index * sz.late_rows, sz.late_rows), sz.late_rows)
    rows_pair = links.in_rows(
        lambda member: b.late_mine.at[few(member)], b.late_in.at[links.row]
    )
    lower.to_line()
    units_middle(0, (0, 1))
    taps_to_line(0)
    units_middle(0, (2,))
    upper.back_line()
    lower.back_line()
    units_end(0, (0,))
    links.wait(rows_pair, b.late_in.at[pl.ds(0, sz.rows - 1)])
    b.late_in[links.row] = b.late_mine[few(links.row), :]
    late = outputs["late"]
    b.late_out[...] = jnp.sum(b.late_in[...].astype(F32), axis=0).astype(BF16)
    place = late.at[few(links.row)]
    ending.append(links.load(b.late_out, place))
    spread_rows = links.in_rows(lambda member: b.late_out, place)
    units_end(0, (1,))
    upper.back_plane()
    units_end(0, (2,))
    lower.back_plane()
    upper.spread.middle()
    lower.spread.middle()
    taps_to_plane(0)
    ending += [upper.finish(), lower.finish()]
    for layer, kind, pair in units_moving:
        links.wait(pair, outputs["units"].at[layer, kind, pl.ds(0, sz.group - 1)])
    links.wait(spread_rows, late.at[pl.ds(0, (sz.rows - 1) * sz.late_rows)])
    for layer, pair in taps_moving.items():
        links.wait(pair, outputs["taps"].at[layer, pl.ds(0, sz.peers - 1)])
    for copy in ending:
        done(copy)


def results_kernel(sz, *refs):
    raw, outs, scratch = refs[:7], refs[7:15], refs[15:]
    targets, held = scratch[:7], scratch[7:15]
    hidden_out, grad_in, gain_out, mixer_out, skip_out, taps_out, pair_out, down_out = held
    upper, lower, late, taps, units = targets[2:]
    channels, sems = scratch[15:]
    targets = (hidden_out, grad_in) + targets[2:]
    copies = [
        pltpu.make_async_copy(source, target, sems.at[index])
        for index, (source, target) in enumerate(zip(raw, targets))
    ]
    for copy in reversed(copies):
        copy.start()
    leaving = []

    def leave(index):
        copy = pltpu.make_async_copy(held[index], outs[index], sems.at[7 + index])
        copy.start()
        leaving.append(copy)

    layers = sz.layers
    copies[6].wait()
    for kind in range(3):
        for layer in range(layers):
            for line in range(sz.group):
                lanes = slice(line * sz.part, (line + 1) * sz.part)
                value = units[layer, kind, line].astype(F32)
                if kind < 2:
                    pair_out[layer, kind, :, lanes] = value
                else:
                    down_out[layer, :, lanes] = value
    leave(6)
    leave(7)
    copies[5].wait()
    for layer in range(layers):
        for way in range(3):
            for row in range(sz.rows):
                part = taps[layer, row % sz.peers, row // sz.peers]
                begin = (row // 2) * sz.couple + (row % 2) * sz.big
                size = sz.small if row % 2 else sz.big
                if way < 2:
                    value = part[way * sz.big : way * sz.big + size, :].astype(F32)
                else:
                    line = part[2 * sz.big : 2 * sz.big + 16, :].astype(F32)[0:1, :]
                    value = jnp.transpose(jnp.broadcast_to(line, (LANES, ORDER)))[0:size, :]
                channels[begin : begin + size, :] = value
            turned = jnp.transpose(channels[...])
            if way < 2:
                taps_out[layer, way] = turned
            else:
                skip_out[layer : layer + 1, :] = turned[0:1, :]
    leave(4)
    leave(5)
    for copy in copies[2:5]:
        copy.wait()

    def matrix(payload, place, layer, kind):
        deep = payload.shape[2]
        count = sz.size // deep
        for part in range(count):
            index = place * count + part
            rows = payload[index // sz.group, index % sz.group].astype(F32)
            for block in range(sz.side_blocks):
                mixer_out[layer, kind, block, part * deep : (part + 1) * deep, :] = rows[
                    :, block_of(sz, block)
                ]

    for place, kind in enumerate((2, 0, 1)):
        matrix(upper, place, 1, kind)
    for place, kind in enumerate((2, 1)):
        matrix(lower, place, 0, kind)
    rows = late[0 : sz.size, :].astype(F32)
    for block in range(sz.side_blocks):
        mixer_out[0, 0, block] = rows[:, block_of(sz, block)]
    index = 2 * (sz.size // sz.deeps[1])
    gains = lower[index // sz.group, index % sz.group].astype(F32)
    gain_out[0, 0:1, :] = late[sz.size : sz.size + 16, :].astype(F32)[0:1, :]
    for row in range(1, 2 * layers):
        gain_out[row // 2, row % 2 : row % 2 + 1, :] = gains[row - 1 : row, :]
    leave(2)
    leave(3)
    for index in range(2):
        copies[index].wait()
        leave(index)
    for copy in leaving:
        copy.wait()


def results(sz, *arrays):
    layers = sz.layers
    outs = (
        ((2 * sz.own, sz.half), BF16),
        ((2 * sz.own, sz.half), F32),
        ((layers, 2, sz.half), F32),
        ((layers, 3, sz.side_blocks, sz.size, sz.size), F32),
        ((layers, sz.half), F32),
        ((layers, 2, ORDER, sz.half), F32),
        ((layers, 2, sz.depth, sz.units), F32),
        ((layers, sz.depth, sz.units), F32),
    )
    anywhere = pl.BlockSpec(memory_space=pl.ANY)
    return pl.pallas_call(
        functools.partial(results_kernel, sz),
        out_shape=tuple(jax.ShapeDtypeStruct(shape, kind) for shape, kind in outs),
        in_specs=[anywhere] * len(arrays),
        out_specs=(anywhere,) * len(outs),
        scratch_shapes=[pltpu.VMEM(entry.shape, entry.dtype) for entry in arrays]
        + [pltpu.VMEM(shape, kind) for shape, kind in outs]
        + [pltpu.VMEM((sz.half, ORDER), F32), pltpu.SemaphoreType.DMA((15,))],
        compiler_params=pltpu.CompilerParams(vmem_limit_bytes=62 * MIB),
        name="results",
    )(*arrays)


def program(sz, arrays):
    names, scratch = layout(sz)
    outs = (
        ((2 * sz.own, sz.half), BF16),
        ((2 * sz.own, sz.half), F32),
        ((sz.peers, sz.group, sz.deeps[0], sz.half), BF16),
        ((sz.peers, sz.group, sz.deeps[1], sz.half), BF16),
        ((sz.rows * sz.late_rows, sz.half), BF16),
        ((sz.layers, sz.peers, sz.group, sz.taps_rows, ORDER), BF16),
        ((sz.layers, 3, sz.group, sz.deep, sz.part), BF16),
    )
    return pl.pallas_call(
        functools.partial(program_kernel, sz),
        out_shape=tuple(jax.ShapeDtypeStruct(shape, kind) for shape, kind in outs),
        in_specs=[pl.BlockSpec(memory_space=pl.ANY)] * len(arrays),
        out_specs=(pl.BlockSpec(memory_space=pl.ANY),) * len(outs),
        scratch_shapes=scratch
        + [pltpu.SemaphoreType.DMA((220,)), pltpu.SemaphoreType.DMA((80,))],
        compiler_params=pltpu.CompilerParams(
            collective_id=0, has_side_effects=True, vmem_limit_bytes=63 * MIB
        ),
        name="program",
    )(*arrays)


def together(sz, hidden_in, d_out, gains, mixer, skip, filters, gate_up, down):
    pos = jnp.asarray(position_table(sz.length).T, F32).astype(BF16)
    arrays = (hidden_in, d_out, gains, mixer, skip, filters, gate_up, down, pos)
    raw = program(sz, arrays + dft_tables(sz.length))

    return results(sz, *raw)


def apart_enter(count, hid):
    me = lax.axis_index("rows") * hid + lax.axis_index("hid")
    barrier = pltpu.get_barrier_semaphore()

    def greet(step, carry):
        peer = lax.rem(me + step, count)
        pl.semaphore_signal(
            barrier, inc=1, device_id=(peer // hid, lax.rem(peer, hid)), device_id_type=MESH
        )
        return carry

    lax.fori_loop(1, count, greet, 0)
    return barrier


def apart_exchange_start(source, target, sems, count, rows, hid, piece, by_owner):
    send, recv, local = sems
    row = lax.axis_index("rows")
    col = lax.axis_index("hid")
    token_id = row * hid + col
    owner_id = col * rows + row
    mine_there = token_id if by_owner else owner_id
    mine_here = owner_id if by_owner else token_id
    at = lambda index: pl.ds(pl.multiple_of(index * piece, piece), piece)
    pltpu.make_async_copy(source.at[at(mine_here)], target.at[at(mine_there)], local).start()

    def post(step, carry):
        peer = lax.rem(token_id + step, count)
        peer_row = peer // hid
        peer_col = lax.rem(peer, hid)
        there = (peer_col * rows + peer_row) if by_owner else peer
        pltpu.make_async_remote_copy(
            src_ref=source.at[at(there)],
            dst_ref=target.at[at(mine_there)],
            send_sem=send,
            recv_sem=recv,
            device_id=(peer_row, peer_col),
            device_id_type=MESH,
        ).start()
        return carry

    lax.fori_loop(1, count, post, 0)


def apart_exchange_wait(source, target, sems, count, rows, hid, piece):
    send, recv, local = sems
    row = lax.axis_index("rows")
    col = lax.axis_index("hid")
    pltpu.make_async_copy(
        source.at[pl.ds(0, piece)], target.at[pl.ds(0, piece)], local
    ).wait()
    span = pl.ds(0, (count - 1) * piece)
    pltpu.make_async_remote_copy(
        src_ref=source.at[span],
        dst_ref=target.at[span],
        send_sem=send,
        recv_sem=recv,
        device_id=(row, hid - 1 - col),
        device_id_type=MESH,
    ).wait()


class apart_Sizes:
    def __init__(self, rows, hid, width, hidden, tokens):
        self.rows, self.hid, self.width, self.hidden = rows, hid, width, hidden
        self.count = rows * hid
        self.chans = width // self.count
        self.piece = round_up(self.chans, 16)
        self.length = min(SEQ_LEN, tokens)
        self.seqs = tokens // self.length
        self.blocks = self.length // LANES
        self.outer = 2 * self.blocks
        self.pairs = self.seqs * self.chans
        self.half = width // hid
        self.padded = rows * self.piece
        self.channels = self.count * self.piece


def apart_spread_in(source, wide, lines, stride, blocks):
    for place, line in enumerate(lines):
        wide[:, place * LANES : (place + 1) * LANES] = source[
            pl.ds(line, blocks, stride=stride), :
        ].astype(wide.dtype)


def apart_dft(wide, spectrum, tables, mid, flat, lines, outer, offset=0):
    outer_fwd, inner_fwd, twist = tables
    mid[:, : lines * LANES] = nn(outer_fwd[...], wide[:, : lines * LANES])
    cos = twist[:, :LANES]
    sin = twist[:, LANES:]
    for line in range(lines):
        lanes = pl.ds(line * LANES, LANES)
        real = mid[0:outer, lanes]
        imag = mid[outer : 2 * outer, lanes]
        rows = pl.ds(line * outer, outer)
        flat[rows, 0:LANES] = (real * cos + imag * sin).astype(BF16)
        flat[rows, LANES:] = (imag * cos - real * sin).astype(BF16)
    spectrum[0 : lines * outer, :] = nn(flat[0 : lines * outer, :], inner_fwd[...])


def apart_inverse_dft(flat, tables, mid_half, lines, outer):
    outer_inv, inner_inv, twist = tables
    cos = twist[:, :LANES]
    sin = twist[:, LANES:]
    for line in range(lines):
        rows = pl.ds(line * outer, outer)
        lanes = pl.ds(line * LANES, LANES)
        part = nn(flat[rows, :], inner_inv[...])
        real = part[:, :LANES]
        imag = part[:, LANES:]
        mid_half[0:outer, lanes] = (real * cos - imag * sin).astype(BF16)
        mid_half[outer : 2 * outer, lanes] = (imag * cos + real * sin).astype(BF16)
    return nn(outer_inv[...], mid_half[:, : lines * LANES])


def apart_spread_out(value, target, lines, stride, blocks):
    for place, line in enumerate(lines):
        target[pl.ds(line, blocks, stride=stride), :] = value[
            :, place * LANES : (place + 1) * LANES
        ]


def apart_signal_lines(sz):
    return [seq * sz.blocks * sz.piece + chan for seq in range(sz.seqs) for chan in range(sz.chans)]


def apart_conv_forward_kernel(
    sz,
    inner_ref,
    taps_ref,
    pos_ref,
    env_ref,
    outer_fwd,
    outer_inv,
    inner_fwd,
    inner_inv,
    twist,
    conv_ref,
    filt_spec,
    sig_spec,
    landed,
    staged,
    tall,
    wide,
    mid,
    flat,
    mid_half,
    sems_in,
    sems_out,
):
    barrier = apart_enter(sz.count, sz.hid)
    pl.semaphore_wait(barrier, sz.count - 1)
    into = tuple(sems_in.at[i] for i in range(3))
    back = tuple(sems_out.at[i] for i in range(3))
    apart_exchange_start(inner_ref, landed, into, sz.count, sz.rows, sz.hid, sz.piece, True)

    piece, blocks, outer = sz.piece, sz.blocks, sz.outer
    step = 4
    for start in range(0, blocks, step):
        span = slice(start * LANES, (start + step) * LANES)
        raw = nn(taps_ref[...], pos_ref[:, span])
        kernels = raw * env_ref[:, span]
        for block in range(step):
            tall[pl.ds((start + block) * 2 * piece, 2 * piece), :] = kernels[
                :, block * LANES : (block + 1) * LANES
            ]
    lines = [way * piece + chan for way in range(2) for chan in range(sz.chans)]
    apart_spread_in(tall, wide, lines, 2 * piece, blocks)
    apart_dft(wide, sig_spec, (outer_fwd, inner_fwd, twist), mid, flat, len(lines), outer)
    span = sz.chans * outer
    filt_spec[:, :LANES] = sig_spec[0:span, :LANES] + sig_spec[span : 2 * span, :LANES]
    filt_spec[:, LANES:] = sig_spec[0:span, LANES:] - sig_spec[span : 2 * span, LANES:]

    apart_exchange_wait(inner_ref, landed, into, sz.count, sz.rows, sz.hid, piece)
    tall[0 : sz.channels, :] = landed[...].astype(F32)
    lines = apart_signal_lines(sz)
    apart_spread_in(tall, wide, lines, piece, blocks)
    apart_dft(wide, sig_spec, (outer_fwd, inner_fwd, twist), mid, flat, sz.pairs, outer)
    for seq in range(sz.seqs):
        rows = pl.ds(seq * span, span)
        sig_re, sig_im = sig_spec[rows, :LANES], sig_spec[rows, LANES:]
        fil_re, fil_im = filt_spec[:, :LANES], filt_spec[:, LANES:]
        flat[rows, :LANES] = (sig_re * fil_re - sig_im * fil_im).astype(BF16)
        flat[rows, LANES:] = (sig_re * fil_im + sig_im * fil_re).astype(BF16)
    result = apart_inverse_dft(flat, (outer_inv, inner_inv, twist), mid_half, sz.pairs, outer)
    apart_spread_out(result, tall, lines, piece, blocks)
    staged[...] = tall[0 : sz.channels, :].astype(BF16)
    apart_exchange_start(staged, conv_ref, back, sz.count, sz.rows, sz.hid, piece, False)
    apart_exchange_wait(staged, conv_ref, back, sz.count, sz.rows, sz.hid, piece)


def apart_conv_forward(sz, inner, taps, pos, env, tables, cid):
    outer_fwd, outer_inv, inner_fwd, inner_inv, twist = tables
    wide_lines = max(2 * sz.chans, sz.pairs)
    return pl.pallas_call(
        functools.partial(apart_conv_forward_kernel, sz),
        out_shape=(
            jax.ShapeDtypeStruct((sz.channels, LANES), BF16),
            jax.ShapeDtypeStruct((sz.chans * sz.outer, 2 * LANES), F32),
            jax.ShapeDtypeStruct((wide_lines * sz.outer, 2 * LANES), F32),
        ),
        in_specs=[whole()] * 9,
        out_specs=(whole(),) * 3,
        scratch_shapes=[
            pltpu.VMEM((sz.channels, LANES), BF16),
            pltpu.VMEM((sz.channels, LANES), BF16),
            pltpu.VMEM((max(2 * sz.piece * sz.blocks, sz.channels), LANES), F32),
            pltpu.VMEM((sz.blocks, wide_lines * LANES), BF16),
            pltpu.VMEM((2 * sz.outer, wide_lines * LANES), F32),
            pltpu.VMEM((wide_lines * sz.outer, 2 * LANES), BF16),
            pltpu.VMEM((2 * sz.outer, sz.pairs * LANES), BF16),
            pltpu.SemaphoreType.DMA((3,)),
            pltpu.SemaphoreType.DMA((3,)),
        ],
        compiler_params=pltpu.CompilerParams(
            collective_id=cid, has_side_effects=True, vmem_limit_bytes=48 * MIB
        ),
        name="conv_forward",
    )(inner, taps, pos, env, outer_fwd, outer_inv, inner_fwd, inner_inv, twist)


def apart_conv_backward_kernel(
    sz,
    grad_ref,
    filt_spec,
    sig_spec,
    taps_ref,
    pos_ref,
    env_ref,
    outer_fwd,
    outer_inv,
    inner_fwd,
    inner_inv,
    twist,
    back_ref,
    taps_grad,
    landed,
    staged,
    tall,
    wide,
    mid,
    flat,
    mid_half,
    grad_spec,
    sems_in,
    sems_out,
):
    barrier = apart_enter(sz.count, sz.hid)
    pl.semaphore_wait(barrier, sz.count - 1)
    into = tuple(sems_in.at[i] for i in range(3))
    back = tuple(sems_out.at[i] for i in range(3))
    piece, blocks, outer = sz.piece, sz.blocks, sz.outer
    apart_exchange_start(grad_ref, landed, into, sz.count, sz.rows, sz.hid, piece, True)
    apart_exchange_wait(grad_ref, landed, into, sz.count, sz.rows, sz.hid, piece)
    tall[0 : sz.channels, :] = landed[...].astype(F32)
    lines = apart_signal_lines(sz)
    apart_spread_in(tall, wide, lines, piece, blocks)
    apart_dft(wide, grad_spec, (outer_fwd, inner_fwd, twist), mid, flat, sz.pairs, outer)
    span = sz.chans * outer
    for seq in range(sz.seqs):
        rows = pl.ds(seq * span, span)
        re, im = grad_spec[rows, :LANES], grad_spec[rows, LANES:]
        fil_re, fil_im = filt_spec[:, :LANES], filt_spec[:, LANES:]
        flat[rows, :LANES] = (re * fil_re + im * fil_im).astype(BF16)
        flat[rows, LANES:] = (im * fil_re - re * fil_im).astype(BF16)
    inv_tables = (outer_inv, inner_inv, twist)
    result = apart_inverse_dft(flat, inv_tables, mid_half, sz.pairs, outer)
    apart_spread_out(result, tall, lines, piece, blocks)
    staged[...] = tall[0 : sz.channels, :].astype(BF16)
    apart_exchange_start(staged, back_ref, back, sz.count, sz.rows, sz.hid, piece, False)

    total_re = jnp.zeros((span, LANES), F32)
    total_im = jnp.zeros((span, LANES), F32)
    for seq in range(sz.seqs):
        rows = pl.ds(seq * span, span)
        re, im = grad_spec[rows, :LANES], grad_spec[rows, LANES:]
        sig_re, sig_im = sig_spec[rows, :LANES], sig_spec[rows, LANES:]
        total_re += re * sig_re + im * sig_im
        total_im += im * sig_re - re * sig_im
    flat[0:span, :LANES] = total_re.astype(BF16)
    flat[span : 2 * span, :LANES] = total_re.astype(BF16)
    flat[0:span, LANES:] = total_im.astype(BF16)
    flat[span : 2 * span, LANES:] = (-total_im).astype(BF16)
    result = apart_inverse_dft(flat, inv_tables, mid_half, 2 * sz.chans, outer)
    lines = [way * piece + chan for way in range(2) for chan in range(sz.chans)]
    if sz.chans < piece:
        tall[...] = jnp.zeros_like(tall)
    apart_spread_out(result, tall, lines, 2 * piece, blocks)
    total = jnp.zeros((2 * piece, ORDER), F32)
    step = 4
    for start in range(0, blocks, step):
        span = slice(start * LANES, (start + step) * LANES)
        raw = nn(taps_ref[...], pos_ref[:, span])
        grads = jnp.concatenate(
            [
                tall[pl.ds((start + block) * 2 * piece, 2 * piece), :]
                for block in range(step)
            ],
            axis=1,
        )
        grads = grads * env_ref[:, span] + (2.0 * DECAY) * raw
        total += nt(grads.astype(BF16), pos_ref[:, span])
    taps_grad[...] = total

    apart_exchange_wait(staged, back_ref, back, sz.count, sz.rows, sz.hid, piece)


def apart_conv_backward(sz, grad, filt_spec, sig_spec, taps, pos, env, tables, cid):
    outer_fwd, outer_inv, inner_fwd, inner_inv, twist = tables
    wide_lines = max(2 * sz.chans, sz.pairs)
    return pl.pallas_call(
        functools.partial(apart_conv_backward_kernel, sz),
        out_shape=(
            jax.ShapeDtypeStruct((sz.channels, LANES), BF16),
            jax.ShapeDtypeStruct((2 * sz.piece, ORDER), F32),
        ),
        in_specs=[whole()] * 11,
        out_specs=(whole(),) * 2,
        scratch_shapes=[
            pltpu.VMEM((sz.channels, LANES), BF16),
            pltpu.VMEM((sz.channels, LANES), BF16),
            pltpu.VMEM((max(2 * sz.piece * sz.blocks, sz.channels), LANES), F32),
            pltpu.VMEM((sz.blocks, wide_lines * LANES), BF16),
            pltpu.VMEM((2 * sz.outer, wide_lines * LANES), F32),
            pltpu.VMEM((wide_lines * sz.outer, 2 * LANES), BF16),
            pltpu.VMEM((2 * sz.outer, wide_lines * LANES), BF16),
            pltpu.VMEM((sz.pairs * sz.outer, 2 * LANES), F32),
            pltpu.SemaphoreType.DMA((3,)),
            pltpu.SemaphoreType.DMA((3,)),
        ],
        compiler_params=pltpu.CompilerParams(
            collective_id=cid, has_side_effects=True, vmem_limit_bytes=48 * MIB
        ),
        name="conv_backward",
    )(grad, filt_spec, sig_spec, taps, pos, env, outer_fwd, outer_inv, inner_fwd, inner_inv, twist)


def apart_project(sz, normed, w_in, w_gate, inner_ref, gate_ref):
    for side in range(sz.hid):
        rows = slice(side * sz.padded, (side + 1) * sz.padded)
        part = normed[:, side * sz.half : (side + 1) * sz.half]
        inner_ref[rows, :] = nt(w_in[side], part).astype(BF16)
        gate_ref[rows, :] = nt(w_gate[side], part)


def apart_first_kernel(sz, x_ref, gain_ref, w_in, w_gate, normed_ref, inner_ref, gate_ref):
    normal, _ = normalize(x_ref[...].astype(F32))
    normed = (normal * gain_ref[0:1, :]).astype(BF16)
    normed_ref[...] = normed
    apart_project(sz, normed, w_in, w_gate, inner_ref, gate_ref)


def apart_first(sz, x, gains, w_in, w_gate):
    tokens = x.shape[0]
    return pl.pallas_call(
        functools.partial(apart_first_kernel, sz),
        out_shape=(
            jax.ShapeDtypeStruct((tokens, sz.width), BF16),
            jax.ShapeDtypeStruct((sz.channels, tokens), BF16),
            jax.ShapeDtypeStruct((sz.channels, tokens), F32),
        ),
        in_specs=[whole()] * 4,
        out_specs=(whole(),) * 3,
        compiler_params=pltpu.CompilerParams(vmem_limit_bytes=32 * MIB),
        name="first_projection",
    )(x, gains, w_in, w_gate)


def apart_mix_out(sz, mixed, w_out):
    parts = []
    for side in range(sz.hid):
        rows = slice(side * sz.padded, (side + 1) * sz.padded)
        parts.append(tn(mixed[rows, :], w_out[side]))
    return jnp.concatenate(parts, axis=1)


def apart_ff_specs(sz, layer, tile):
    steps = sz.hidden // sz.hid // tile
    first_half = lambda i: jnp.minimum(i, steps - 1)
    second = lambda i: jnp.maximum(i - steps, 0)
    specs = []
    for place in (first_half, second):
        specs.append(
            pl.BlockSpec((1, 2, sz.width, tile), lambda i, place=place: (layer, 0, 0, place(i)))
        )
        specs.append(pl.BlockSpec((1, sz.width, tile), lambda i, place=place: (layer, 0, place(i))))
    return specs, steps


def apart_forward_kernel(
    sz,
    steps,
    conv_ref,
    inner_ref,
    gate_ref,
    skip_ref,
    x_ref,
    gain_ref,
    next_gain,
    w_out,
    w_in,
    w_gate,
    up_a,
    down_a,
    up_b,
    down_b,
    summed_ref,
    mixed_ref,
    middle_ref,
    normed_two,
    next_x,
    next_normed,
    next_inner,
    next_gate,
):
    index = pl.program_id(0)

    @pl.when(index == 0)
    def _():
        summed = conv_ref[...].astype(F32) + skip_ref[...] * inner_ref[...].astype(F32)
        summed_ref[...] = summed
        mixed_ref[...] = (gate_ref[...] * summed).astype(BF16)
        middle = x_ref[...].astype(F32) + apart_mix_out(sz, mixed_ref, w_out)
        middle_ref[...] = middle
        normal, _ = normalize(middle)
        normed_two[...] = (normal * gain_ref[1:2, :]).astype(BF16)
        next_x[...] = middle

    def accumulate(up_ref, down_ref):
        gate = nn(normed_two[...], up_ref[0, 0])
        up = nn(normed_two[...], up_ref[0, 1])
        value, _ = gelu_parts(gate)
        next_x[...] += nt((value * up).astype(BF16), down_ref[0])

    pl.when(index < steps)(lambda: accumulate(up_a, down_a))
    pl.when(index >= steps)(lambda: accumulate(up_b, down_b))

    @pl.when(index == 2 * steps - 1)
    def _():
        normal, _ = normalize(next_x[...])
        normed = (normal * next_gain[0:1, :]).astype(BF16)
        next_normed[...] = normed
        apart_project(sz, normed, w_in, w_gate, next_inner, next_gate)


def apart_full(shape):
    return pl.BlockSpec(shape, lambda i: (0,) * len(shape))


def apart_forward(sz, layer, conv, inner, gate, skip, x, gains, next_gains, w_out, w_in, w_gate, ff):
    tokens = x.shape[0]
    tile = 512
    specs, steps = apart_ff_specs(sz, layer, tile)
    small = (conv, inner, gate, skip, x, gains, next_gains, w_out, w_in, w_gate)
    outs = (
        ((sz.channels, tokens), F32),
        ((sz.channels, tokens), BF16),
        ((tokens, sz.width), F32),
        ((tokens, sz.width), BF16),
        ((tokens, sz.width), F32),
        ((tokens, sz.width), BF16),
        ((sz.channels, tokens), BF16),
        ((sz.channels, tokens), F32),
    )
    return pl.pallas_call(
        functools.partial(apart_forward_kernel, sz, steps),
        grid=(2 * steps,),
        out_shape=tuple(jax.ShapeDtypeStruct(shape, kind) for shape, kind in outs),
        in_specs=[apart_full(entry.shape) for entry in small] + specs,
        out_specs=tuple(apart_full(shape) for shape, kind in outs),
        compiler_params=pltpu.CompilerParams(
            dimension_semantics=("arbitrary",), vmem_limit_bytes=48 * MIB
        ),
        name="token_forward",
    )(*small, *ff)


def apart_block_grads(sz, tall, flat, target, slot):
    blocks_side = target.shape[1] // sz.hid
    size = sz.half // blocks_side
    rows = sz.padded // blocks_side
    for side in range(sz.hid):
        for block in range(blocks_side):
            begin = side * sz.padded + block * rows
            place = side * sz.half + block * size
            target[slot, side * blocks_side + block] = nn(
                tall[begin : begin + rows, :], flat[:, place : place + size]
            ).astype(target.dtype)


def apart_ff_backward_tile(normed, grad, up_ref, down_ref, total, out_total):
    gate = nn(normed, up_ref[0, 0])
    up = nn(normed, up_ref[0, 1])
    grad_hidden = nn(grad, down_ref[0])
    value, slope = gelu_parts(gate)
    if out_total is not None:
        out_total[...] += nt((value * up).astype(BF16), down_ref[0])
    grad_gate = (slope * up * grad_hidden).astype(BF16)
    grad_up = (value * grad_hidden).astype(BF16)
    total[...] += nt(grad_gate, up_ref[0, 0]) + nt(grad_up, up_ref[0, 1])


def apart_mixer_backward(
    sz, grad_next, middle, total, gain, mixed, summed, gate, w_out, outs
):
    grad_middle, mixer_grad, grad_gate, grad_summed, grad_conv, gain_grad = outs
    normal, inv = normalize(middle)
    back, gain_grad[...] = norm_back(total, normal, inv, gain)
    result = grad_next + back
    grad_middle[...] = result
    grad_o = result.astype(BF16)
    apart_block_grads(sz, mixed, grad_o, mixer_grad, 0)
    for side in range(sz.hid):
        rows = slice(side * sz.padded, (side + 1) * sz.padded)
        grad_mixed = nt(w_out[side], grad_o[:, side * sz.half : (side + 1) * sz.half])
        grad_gate[rows, :] = (grad_mixed * summed[rows, :]).astype(BF16)
        through = grad_mixed * gate[rows, :]
        grad_summed[rows, :] = through
        grad_conv[rows, :] = through.astype(BF16)


def apart_mixer_outs(sz, tokens, blocks):
    size = sz.width // blocks
    return (
        ((tokens, sz.width), F32),
        ((1, blocks, sz.channels // blocks, size), BF16),
        ((sz.channels, tokens), BF16),
        ((sz.channels, tokens), F32),
        ((sz.channels, tokens), BF16),
        ((1, sz.width), F32),
    )


def apart_turn_kernel(
    sz,
    steps,
    conv_ref,
    inner_ref,
    gate_ref,
    skip_ref,
    x_ref,
    gain_ref,
    grad_ref,
    w_out,
    up_a,
    down_a,
    up_b,
    down_b,
    hidden_out,
    normed_two,
    grad_middle,
    mixer_grad,
    grad_gate,
    grad_summed,
    grad_conv,
    gain_grad,
    summed,
    mixed,
    middle,
    out_total,
    total,
):
    index = pl.program_id(0)

    @pl.when(index == 0)
    def _():
        summed[...] = conv_ref[...].astype(F32) + skip_ref[...] * inner_ref[...].astype(F32)
        mixed[...] = (gate_ref[...] * summed[...]).astype(BF16)
        middle[...] = x_ref[...].astype(F32) + apart_mix_out(sz, mixed, w_out)
        normal, _ = normalize(middle[...])
        normed_two[...] = (normal * gain_ref[1:2, :]).astype(BF16)
        out_total[...] = middle[...]
        total[...] = jnp.zeros_like(total)

    def accumulate(up_ref, down_ref):
        apart_ff_backward_tile(normed_two[...], grad_ref[...], up_ref, down_ref, total, out_total)

    pl.when(index < steps)(lambda: accumulate(up_a, down_a))
    pl.when(index >= steps)(lambda: accumulate(up_b, down_b))

    @pl.when(index == 2 * steps - 1)
    def _():
        hidden_out[...] = out_total[...].astype(BF16)
        outs = (grad_middle, mixer_grad, grad_gate, grad_summed, grad_conv, gain_grad)
        apart_mixer_backward(
            sz,
            grad_ref[...].astype(F32),
            middle[...],
            total[...],
            gain_ref[1:2, :],
            mixed,
            summed,
            gate_ref,
            w_out,
            outs,
        )


def apart_turn(sz, layer, blocks, conv, inner, gate, skip, x, gains, grad, w_out, ff):
    tokens = x.shape[0]
    specs, steps = apart_ff_specs(sz, layer, 512)
    small = (conv, inner, gate, skip, x, gains, grad, w_out)
    outs = (((tokens, sz.width), BF16), ((tokens, sz.width), BF16)) + apart_mixer_outs(sz, tokens, blocks)
    return pl.pallas_call(
        functools.partial(apart_turn_kernel, sz, steps),
        grid=(2 * steps,),
        out_shape=tuple(jax.ShapeDtypeStruct(shape, kind) for shape, kind in outs),
        in_specs=[apart_full(entry.shape) for entry in small] + specs,
        out_specs=tuple(apart_full(shape) for shape, kind in outs),
        scratch_shapes=[
            pltpu.VMEM((sz.channels, tokens), F32),
            pltpu.VMEM((sz.channels, tokens), BF16),
            pltpu.VMEM((tokens, sz.width), F32),
            pltpu.VMEM((tokens, sz.width), F32),
            pltpu.VMEM((tokens, sz.width), F32),
        ],
        compiler_params=pltpu.CompilerParams(
            dimension_semantics=("arbitrary",), vmem_limit_bytes=48 * MIB
        ),
        name="token_turn",
    )(*small, *ff)


def apart_input_backward(
    sz, back, through, grad_gate, skip, normed, x, gain, w_in, w_gate, grad_middle, mixer_grad
):
    inner_grad = (skip * through + back.astype(F32)).astype(BF16)
    apart_block_grads(sz, inner_grad, normed, mixer_grad, 0)
    apart_block_grads(sz, grad_gate, normed, mixer_grad, 1)
    parts = []
    for side in range(sz.hid):
        rows = slice(side * sz.padded, (side + 1) * sz.padded)
        parts.append(tn(inner_grad[rows, :], w_in[side]) + tn(grad_gate[rows, :], w_gate[side]))
    normal, inv = normalize(x)
    result, gain_grad = norm_back(jnp.concatenate(parts, axis=1), normal, inv, gain)
    return grad_middle + result, gain_grad


def apart_backward_kernel(
    sz,
    steps,
    back_ref,
    through_ref,
    gate_grad_ref,
    skip_ref,
    normed_ref,
    x_ref,
    gain_ref,
    w_in,
    w_gate,
    grad_middle_ref,
    normed_two,
    middle_ref,
    summed_ref,
    gate_ref,
    mixed_ref,
    low_gain,
    w_out,
    up_a,
    down_a,
    up_b,
    down_b,
    input_grad,
    input_gain,
    grad_ff,
    grad_middle,
    mixer_grad,
    grad_gate,
    grad_summed,
    grad_conv,
    gain_grad,
    grad_next,
    total,
):
    index = pl.program_id(0)

    @pl.when(index == 0)
    def _():
        result, input_gain[...] = apart_input_backward(
            sz,
            back_ref[...],
            through_ref[...],
            gate_grad_ref[...],
            skip_ref[...],
            normed_ref[...],
            x_ref[...],
            gain_ref[0:1, :],
            w_in,
            w_gate,
            grad_middle_ref[...],
            input_grad,
        )
        grad_next[...] = result
        grad_ff[...] = result.astype(BF16)
        total[...] = jnp.zeros_like(total)

    def accumulate(up_ref, down_ref):
        apart_ff_backward_tile(normed_two[...], grad_ff[...], up_ref, down_ref, total, None)

    pl.when(index < steps)(lambda: accumulate(up_a, down_a))
    pl.when(index >= steps)(lambda: accumulate(up_b, down_b))

    @pl.when(index == 2 * steps - 1)
    def _():
        outs = (grad_middle, mixer_grad, grad_gate, grad_summed, grad_conv, gain_grad)
        apart_mixer_backward(
            sz,
            grad_next[...],
            middle_ref[...],
            total[...],
            low_gain[1:2, :],
            mixed_ref,
            summed_ref,
            gate_ref,
            w_out,
            outs,
        )


def apart_input_outs(sz, blocks):
    size = sz.width // blocks
    return (((2, blocks, sz.channels // blocks, size), BF16), ((1, sz.width), F32))


def apart_backward(
    sz,
    layer,
    blocks,
    back,
    through,
    gate_grad,
    skip,
    normed,
    x,
    gains,
    w_in,
    w_gate,
    grad_middle,
    normed_two,
    middle,
    summed,
    gate,
    mixed,
    low_gains,
    w_out,
    ff,
):
    tokens = x.shape[0]
    specs, steps = apart_ff_specs(sz, layer, 512)
    small = (
        back,
        through,
        gate_grad,
        skip,
        normed,
        x,
        gains,
        w_in,
        w_gate,
        grad_middle,
        normed_two,
        middle,
        summed,
        gate,
        mixed,
        low_gains,
        w_out,
    )
    outs = (
        apart_input_outs(sz, blocks) + (((tokens, sz.width), BF16),) + apart_mixer_outs(sz, tokens, blocks)
    )
    return pl.pallas_call(
        functools.partial(apart_backward_kernel, sz, steps),
        grid=(2 * steps,),
        out_shape=tuple(jax.ShapeDtypeStruct(shape, kind) for shape, kind in outs),
        in_specs=[apart_full(entry.shape) for entry in small] + specs,
        out_specs=tuple(apart_full(shape) for shape, kind in outs),
        scratch_shapes=[
            pltpu.VMEM((tokens, sz.width), F32),
            pltpu.VMEM((tokens, sz.width), F32),
        ],
        compiler_params=pltpu.CompilerParams(
            dimension_semantics=("arbitrary",), vmem_limit_bytes=48 * MIB
        ),
        name="token_backward",
    )(*small, *ff)


def apart_last_kernel(
    sz,
    back_ref,
    through_ref,
    gate_grad_ref,
    skip_ref,
    normed_ref,
    x_ref,
    gain_ref,
    w_in,
    w_gate,
    grad_middle_ref,
    input_grad,
    input_gain,
    grad_in,
):
    grad_in[...], input_gain[...] = apart_input_backward(
        sz,
        back_ref[...],
        through_ref[...],
        gate_grad_ref[...],
        skip_ref[...],
        normed_ref[...],
        x_ref[...].astype(F32),
        gain_ref[0:1, :],
        w_in,
        w_gate,
        grad_middle_ref[...],
        input_grad,
    )


def apart_last(sz, blocks, *args):
    tokens = args[5].shape[0]
    outs = apart_input_outs(sz, blocks) + (((tokens, sz.width), F32),)
    return pl.pallas_call(
        functools.partial(apart_last_kernel, sz),
        out_shape=tuple(jax.ShapeDtypeStruct(shape, kind) for shape, kind in outs),
        in_specs=[whole()] * len(args),
        out_specs=(whole(),) * len(outs),
        compiler_params=pltpu.CompilerParams(vmem_limit_bytes=32 * MIB),
        name="last_projection",
    )(*args)


def apart_ff_grads_kernel(normed_ref, grad_ref, up_ref, down_ref, out_ref, hidden, grad_gate, grad_up):
    tokens = normed_ref.shape[0]
    chunk = 256
    for start in range(0, tokens, chunk):
        rows = pl.ds(start, chunk)
        normed = normed_ref[rows, :]
        gate = nn(normed, up_ref[0])
        up = nn(normed, up_ref[1])
        through = nn(grad_ref[rows, :], down_ref[...])
        value, slope = gelu_parts(gate)
        hidden[rows, :] = (value * up).astype(BF16)
        grad_gate[rows, :] = (slope * up * through).astype(BF16)
        grad_up[rows, :] = (value * through).astype(BF16)
    out_ref[0] = tn(normed_ref[...], grad_gate[...]).astype(BF16)
    out_ref[1] = tn(normed_ref[...], grad_up[...]).astype(BF16)
    out_ref[2] = tn(grad_ref[...], hidden[...]).astype(BF16)


def apart_ff_grads(normed, grad, up, down):
    tokens, width = normed.shape
    units = down.shape[1]
    return pl.pallas_call(
        apart_ff_grads_kernel,
        out_shape=jax.ShapeDtypeStruct((3, width, units), BF16),
        in_specs=[whole()] * 4,
        out_specs=whole(),
        scratch_shapes=[pltpu.VMEM((tokens, units), BF16)] * 3,
        compiler_params=pltpu.CompilerParams(vmem_limit_bytes=48 * MIB),
        name="ff_weight_grads",
    )(normed, grad, up, down)


def apart_row_exchange_kernel(rows, parts, *refs):
    sources, targets, sems = refs[:parts], refs[parts : 2 * parts], refs[2 * parts]
    row = lax.axis_index("rows")
    col = lax.axis_index("hid")
    barrier = pltpu.get_barrier_semaphore()

    def greet(step, carry):
        peer = lax.rem(row + step, rows)
        pl.semaphore_signal(barrier, inc=1, device_id=(peer, col), device_id_type=MESH)
        return carry

    lax.fori_loop(1, rows, greet, 0)
    for part in range(parts):
        pltpu.make_async_copy(
            sources[part].at[row], targets[part].at[row], sems.at[part, 2]
        ).start()
    pl.semaphore_wait(barrier, rows - 1)

    def post(step, carry):
        peer = lax.rem(row + step, rows)
        for part in range(parts):
            pltpu.make_async_remote_copy(
                src_ref=sources[part].at[peer],
                dst_ref=targets[part].at[row],
                send_sem=sems.at[part, 0],
                recv_sem=sems.at[part, 1],
                device_id=(peer, col),
                device_id_type=MESH,
            ).start()
        return carry

    lax.fori_loop(1, rows, post, 0)
    for part in range(parts):
        pltpu.make_async_copy(
            sources[part].at[0], targets[part].at[0], sems.at[part, 2]
        ).wait()
        span = pl.ds(0, rows - 1)
        pltpu.make_async_remote_copy(
            src_ref=sources[part].at[span],
            dst_ref=targets[part].at[span],
            send_sem=sems.at[part, 0],
            recv_sem=sems.at[part, 1],
            device_id=(lax.rem(row + 1, rows), col),
            device_id_type=MESH,
        ).wait()


def apart_row_exchange(arrays, rows, cid):
    parts = len(arrays)
    return pl.pallas_call(
        functools.partial(apart_row_exchange_kernel, rows, parts),
        out_shape=tuple(jax.ShapeDtypeStruct(entry.shape, entry.dtype) for entry in arrays),
        in_specs=[pl.BlockSpec(memory_space=pl.ANY)] * parts,
        out_specs=(pl.BlockSpec(memory_space=pl.ANY),) * parts,
        scratch_shapes=[pltpu.SemaphoreType.DMA((parts, 3))],
        compiler_params=pltpu.CompilerParams(collective_id=cid, has_side_effects=True),
        name="row_exchange",
    )(*arrays)


def apart_swap(value):
    return lax.ppermute(value, "hid", [(0, 1), (1, 0)])


def apart_both_halves(own, axis):
    other = apart_swap(own)
    low = lax.axis_index("hid") == 0
    return jnp.concatenate([jnp.where(low, own, other), jnp.where(low, other, own)], axis=axis)


def apart_own_tokens(part):
    tokens = part.shape[0] // 2
    side = lax.axis_index("hid")
    keep = lax.dynamic_slice_in_dim(part, side * tokens, tokens, 0)
    other = apart_swap(lax.dynamic_slice_in_dim(part, (1 - side) * tokens, tokens, 0))
    low = side == 0
    return jnp.concatenate([jnp.where(low, keep, other), jnp.where(low, other, keep)], axis=1)


def apart_own_features(part):
    half = part.shape[1] // 2
    side = lax.axis_index("hid")
    keep = lax.dynamic_slice_in_dim(part, side * half, half, 1)
    other = apart_swap(lax.dynamic_slice_in_dim(part, (1 - side) * half, half, 1))
    low = side == 0
    return jnp.concatenate([jnp.where(low, keep, other), jnp.where(low, other, keep)], axis=0)


def apart_padded_mixer(sz, mixer):
    layers, kinds, blocks, size, _ = mixer.shape
    chan_first = jnp.concatenate([jnp.swapaxes(mixer[:, :2], 3, 4), mixer[:, 2:]], axis=1)
    grouped = chan_first.reshape(layers, kinds, blocks, size // sz.chans, sz.chans, size)
    grouped = jnp.pad(grouped, ((0, 0),) * 4 + ((0, sz.piece - sz.chans), (0, 0)))
    grouped = grouped.reshape(layers, kinds, blocks, -1, size)
    parts = [
        jnp.pad(grouped[:, :, block], ((0, 0),) * 3 + ((block * size, (blocks - 1 - block) * size),))
        for block in range(blocks)
    ]
    return jnp.concatenate(parts, axis=2)


def apart_padded_channels(sz, values):
    lead = values.shape[:-1]
    grouped = values.reshape(lead + (sz.rows, sz.chans))
    grouped = jnp.pad(grouped, ((0, 0),) * (len(lead) + 1) + ((0, sz.piece - sz.chans),))
    return grouped.reshape(lead + (sz.padded,))


def apart_envelopes(sz):
    row = lax.axis_index("rows")
    first_chan = lax.axis_index("hid") * sz.half + row * sz.chans
    channels = first_chan + jnp.arange(sz.piece, dtype=jnp.int32)
    fraction = (channels * 37 % sz.width).astype(F32) / (sz.width - 1)
    start_log = math.log(1.0 / 40.0)
    rate = jnp.exp(start_log + (math.log(1.5 / sz.length) - start_log) * fraction)
    steps = jnp.arange(sz.length, dtype=jnp.int32).astype(F32)
    decay = jnp.exp(-steps[None, :] * rate[:, None])
    shape = decay * lax.rsqrt(2.0 * jnp.sum(decay * decay, axis=1, keepdims=True))
    return jnp.concatenate([shape, shape * (steps > 0)[None, :]], axis=0)


def apart_plane_gather(value):
    size = lax.axis_size("rows")
    for bit in (1, 2):
        other = lax.ppermute(value, "rows", [(r, r ^ bit) for r in range(size)])
        value = jnp.concatenate([value, other], axis=0)
    return jnp.concatenate([value, apart_swap(value)], axis=0)


def apart_on_device(hidden_in, d_out, gains, mixer, skip, filters, gate_up, down):
    layers = gate_up.shape[0]
    rows = lax.axis_size("rows")
    hid = lax.axis_size("hid")
    width = gate_up.shape[2]
    hidden = gate_up.shape[3] * hid
    blocks = mixer.shape[2] * hid
    block_size = mixer.shape[3]
    sz = apart_Sizes(rows, hid, width, hidden, hidden_in.shape[0] * rows)
    row = lax.axis_index("rows")

    x = apart_own_tokens(hidden_in)
    gains_all = apart_both_halves(gains, 2)
    skip_all = apart_both_halves(apart_padded_channels(sz, skip), 1)[:, :, None]
    weights = apart_both_halves(apart_padded_mixer(sz, mixer)[:, :, None], 2)
    gate_up_b = apart_swap(gate_up)
    down_b = apart_swap(down)
    ff = (gate_up, down, gate_up_b, down_b)
    grad_out = apart_own_tokens(d_out)

    tables = dft_tables(sz.length)
    pos = jnp.asarray(position_table(sz.length).T, F32).astype(BF16)
    env = apart_envelopes(sz)
    taps = lax.dynamic_slice_in_dim(filters, row * sz.chans, sz.chans, 3)
    taps = jnp.pad(taps, ((0, 0),) * 3 + ((0, sz.piece - sz.chans),))
    taps = jnp.swapaxes(taps, 2, 3).reshape(layers, 2 * sz.piece, ORDER).astype(BF16)

    normed, inner, gate = apart_first(sz, x, gains_all[0], weights[0, 0], weights[0, 1])
    stored = []
    for layer in range(layers):
        conv, filt_spec, sig_spec = apart_conv_forward(sz, inner, taps[layer], pos, env, tables, 0)
        stored.append(dict(x=x, normed=normed, inner=inner, gate=gate, f=filt_spec, s=sig_spec))
        if layer < layers - 1:
            summed, mixed, middle, normed_two, x, normed, next_inner, next_gate = apart_forward(
                sz,
                layer,
                conv,
                inner,
                gate,
                skip_all[layer],
                x,
                gains_all[layer],
                gains_all[layer + 1],
                weights[layer, 2],
                weights[layer + 1, 0],
                weights[layer + 1, 1],
                ff,
            )
            stored[-1].update(summed=summed, mixed=mixed, middle=middle, normed_two=normed_two)
            inner, gate = next_inner, next_gate

    top = layers - 1
    hidden_out, normed_two, *rest = apart_turn(
        sz,
        top,
        blocks,
        conv,
        inner,
        gate,
        skip_all[top],
        x,
        gains_all[top],
        grad_out,
        weights[top, 2],
        ff,
    )
    stored[top].update(normed_two=normed_two)
    grad_ff = grad_out
    units = sz.hidden // hid // 4
    unit_start = lax.rem(row, 4) * units
    ff_parts, mixer_parts, gain_parts, skip_parts, taps_parts = [], [], [], [], []
    for layer in reversed(range(layers)):
        kept = stored[layer]
        grad_middle, out_grad, grad_gate, grad_summed, grad_conv, gain_two = rest
        ff_parts.insert(
            0,
            apart_ff_grads(
                apart_plane_gather(kept["normed_two"]),
                apart_plane_gather(grad_ff),
                lax.dynamic_slice_in_dim(gate_up[layer], unit_start, units, 2),
                lax.dynamic_slice_in_dim(down[layer], unit_start, units, 1),
            ),
        )
        back, taps_grad = apart_conv_backward(
            sz, grad_conv, kept["f"], kept["s"], taps[layer], pos, env, tables, 1
        )
        skip_parts.insert(0, jnp.sum(grad_summed * kept["inner"].astype(F32), axis=1))
        taps_parts.insert(0, taps_grad)
        common = (
            back,
            grad_summed,
            grad_gate,
            skip_all[layer],
            kept["normed"],
            kept["x"],
            gains_all[layer],
            weights[layer, 0],
            weights[layer, 1],
            grad_middle,
        )
        if layer > 0:
            low = stored[layer - 1]
            in_grad, gain_one, grad_ff, *rest = apart_backward(
                sz,
                layer - 1,
                blocks,
                *common,
                low["normed_two"],
                low["middle"],
                low["summed"],
                low["gate"],
                low["mixed"],
                gains_all[layer - 1],
                weights[layer - 1, 2],
                ff,
            )
        else:
            in_grad, gain_one, grad_in = apart_last(sz, blocks, *common)
        mixer_parts.insert(0, jnp.concatenate([in_grad, out_grad], axis=0))
        gain_parts.insert(0, jnp.concatenate([gain_one, gain_two], axis=0))

    piece_rows = width // rows
    padded_rows = round_up(piece_rows, 16)
    pieces = jnp.stack(ff_parts).reshape(layers, 3, rows, piece_rows, units)
    pieces = jnp.pad(pieces, ((0, 0),) * 3 + ((0, padded_rows - piece_rows), (0, 0)))
    pieces = jnp.moveaxis(pieces, 2, 0)
    (arrived,) = apart_row_exchange((pieces,), rows, 2)
    arrived = arrived.reshape(rows // 4, 4, layers, 3, padded_rows, units)[:, :, :, :, :piece_rows]
    summed_ff = jnp.sum(arrived.astype(F32), axis=0)
    summed_ff = jnp.moveaxis(summed_ff, 0, 3).reshape(layers, 3, piece_rows, 4 * units)

    mixers = jnp.stack(mixer_parts).reshape(layers, 3, blocks, -1, sz.piece, block_size)
    mixers = mixers[:, :, :, :, : sz.chans].reshape(layers, 3, blocks, block_size, block_size)
    small = jnp.concatenate(
        [jnp.stack(gain_parts).reshape(-1), jnp.stack(skip_parts).reshape(-1)]
    )
    mixers, small = lax.psum((mixers.astype(F32), small), ("rows", "hid"))
    side = lax.axis_index("hid")
    mixers = lax.dynamic_slice_in_dim(mixers, side * (blocks // hid), blocks // hid, 2)
    mixers = jnp.concatenate([jnp.swapaxes(mixers[:, :2], 3, 4), mixers[:, 2:]], axis=1)
    gain_size = layers * 2 * width
    gain_out = lax.dynamic_slice_in_dim(
        small[:gain_size].reshape(layers, 2, width), side * sz.half, sz.half, 2
    )
    skip_out = small[gain_size:].reshape(layers, hid, rows, sz.piece)[..., : sz.chans]
    skip_out = lax.dynamic_index_in_dim(skip_out, side, 1, False).reshape(layers, sz.half)
    taps_out = jnp.stack(taps_parts).reshape(layers, 2, sz.piece, ORDER)[:, :, : sz.chans]
    taps_out = lax.all_gather(taps_out, "rows", axis=2, tiled=True)
    return (
        apart_own_features(hidden_out),
        apart_own_features(grad_in),
        gain_out,
        mixers,
        skip_out,
        jnp.swapaxes(taps_out, 2, 3),
        summed_ff[:, :2],
        summed_ff[:, 2],
    )


def on_device(*arrays):
    sz = Sizes.of(*arrays)
    return together(sz, *arrays) if sz.fits() else apart_on_device(*arrays)


def solution(mesh):
    placed = (
        P("rows", "hid"),
        P("rows", "hid"),
        P(None, None, "hid"),
        P(None, None, "hid", None, None),
        P(None, "hid"),
        P(None, None, None, "hid"),
        P(None, None, None, "hid"),
        P(None, None, "hid"),
    )
    return jax.shard_map(
        on_device,
        mesh=mesh,
        in_specs=placed,
        out_specs=(
            P("rows", "hid"),
            P("rows", "hid"),
            P(None, None, "hid"),
            P(None, None, "hid", None, None),
            P(None, "hid"),
            P(None, None, None, "hid"),
            P(None, None, "rows", "hid"),
            P(None, "rows", "hid"),
        ),
        check_vma=False,
    )
```

profile of v0, /device:TPU:0, one launch (start us, length us, event | category | flops | bytes accessed | tf_op | source)
XLA Modules:
  0.0 163.7 jit_solution(4892841692405870015)
XLA Ops:
  0.6 158.7 %program.1 = (bf16[256,384]{1,0:T(8,128)(2,1)}, f32[256,384]{1,0:T(8,128)}, bf16[4,4,48,384]{3,2,1,0:T(8,128)(2,1)}, bf16[4,4,32,384]{3,2,1,0:T(8,128)(2,1)}, bf...) custom-call(bf16[256,384]{1,0:T(8,128)(2,1)} %refs_0_.1, ...), custom_call_target="tpu_custom_call" | custom-call | tf_op jit(solution)/shard_map/program/pallas_call | solution.py:1505
  159.4 4.1 %results.1 = (bf16[256,384]{1,0:T(8,128)(2,1)}, f32[256,384]{1,0:T(8,128)}, f32[2,2,384]{2,1,0:T(2,128)}, f32[2,3,2,192,192]{4,3,2,1,0:T(8,128)}, f32[2,384]{1,0...) custom-call(bf16[256,384]{1,0:T(8,128)(2,1)} %get-tuple-element.15.refs_0_, ...), custom_call_target="tpu_custom_call" | custom-call | tf_op jit(solution)/shard_map/results/pallas_call | solution.py:1481
where the time goes:
time: 164 us
  Pallas kernels  163 us (99%)
    pallas_call x1, Pallas kernels, program(): pl.pallas_call(functools.partial(program_kernel, sz), out_shape=tuple((ja...  159 us
    pallas_call x1, Pallas kernels, results(): pl.pallas_call(functools.partial(results_kernel, sz), out_shape=tuple((ja...  4.12 us

commit v1 on v0

--- a/solution.py
+++ b/solution.py
@@ -116,10 +116,9 @@
         self.depth = width // rows
         self.deep = round_up(self.depth, 16)
         self.deeps = tuple(
-            round_up(-(-rows_needed // rows), 16)
-            for rows_needed in (3 * (layers - 1) * self.size, 2 * self.size + 16)
+            round_up(-(-(matrices * self.size + 16) // rows), 16)
+            for matrices in (3 * layers - 1, 1)
         )
-        self.late_rows = round_up(-(-(self.size + 16) // rows), 16)
         self.taps_rows = round_up(2 * self.big + 1, 16)
 
 
@@ -132,7 +131,7 @@
 
 
     def fits(self):
-        whole_tiles = self.small > 0 and self.small % 16 == 0 and self.rows % 8 == 0
+        whole_tiles = self.small == 16 and self.big == 32 and self.rows % 8 == 0
         whole_tiles = whole_tiles and self.own == LANES and self.depth % 16 == 0
         whole_tiles = whole_tiles and self.peers == 4 and self.layers == 2 and self.seqs == 1
         whole_tiles = whole_tiles and all(self.size % deep == 0 for deep in self.deeps)
@@ -260,6 +259,27 @@
         return lambda member: self.second.at[member // count, lax.rem(member, count)]
 
 
+class DirectSum(Plane):
+    def __init__(self, links, source, parts):
+        super().__init__(links)
+        self.source, self.parts = source, parts
+
+    def start(self):
+        self.pair = self.links.in_plane(self.source, self.parts.at[self.me])
+
+    def end(self):
+        links = self.links
+        links.wait(self.pair, self.parts.at[pl.ds(0, links.sz.peers - 1)])
+
+    def sums(self):
+        self.parts[self.me] = self.source(self.me)[...]
+        total = self.parts[0].astype(F32)
+        for member in range(1, self.links.sz.peers):
+            total += self.parts[member].astype(F32)
+        self.parts[0] = total.astype(BF16)
+        return lambda member: self.parts.at[0, member]
+
+
 class PlaneSpread(Plane):
     def __init__(self, links, place, span):
         super().__init__(links)
@@ -291,6 +311,7 @@
 class Payload:
     def __init__(self, sz, b, links, index, output):
         self.sz, self.links, self.output = sz, links, output
+        self.direct = index == 1
         self.deep = sz.deeps[index]
         for name in LOAD_BUFFERS:
             setattr(self, name, getattr(b, "load_" + name)[index])
@@ -302,6 +323,8 @@
             self.second_give,
             self.second,
         )
+        if self.direct:
+            self.plane = DirectSum(links, lambda member: self.mine.at[member], b.late_parts)
         self.spread = PlaneSpread(
             links,
             lambda member, which: self.got.at[member, half(which)],
@@ -357,11 +380,19 @@
         self.pair = links.in_line(lambda member: self.out, self.got.at[links.plane, links.line])
 
     def back_plane(self):
-        self.links.wait(self.pair, self.got.at[0, pl.ds(0, self.sz.group - 1)])
-        self.spread.start()
+        links = self.links
+        links.wait(self.pair, self.got.at[0, pl.ds(0, self.sz.group - 1)])
+        if self.direct:
+            place = self.got.at[links.plane]
+            self.pair = links.in_plane(lambda member: place, place)
+        else:
+            self.spread.start()
 
     def finish(self):
-        self.spread.end()
+        if self.direct:
+            self.links.wait(self.pair, self.got.at[pl.ds(0, self.sz.peers - 1)])
+        else:
+            self.spread.end()
         return self.links.load(self.got, self.output)
 
 
@@ -389,13 +420,13 @@
         self.odd = lax.rem(links.row, 2)
         self.token = links.row * sz.hid + links.col
 
-    def channels(self, row, col, size):
+    def channels(self, row, col, part):
         sz = self.sz
         start = col * sz.half + (row // 2) * sz.couple + lax.rem(row, 2) * sz.big
-        return pl.ds(pl.multiple_of(start, 16), size)
-
-    def block(self, token, size):
-        return pl.ds(pl.multiple_of(token * self.sz.big, 16), size)
+        return pl.ds(pl.multiple_of(start + part * 16, 16), 16)
+
+    def block(self, token):
+        return pl.ds(pl.multiple_of(token * 16, 16), 16)
 
     def far_first(self):
         line = self.links.line
@@ -403,9 +434,11 @@
         across = 2 * (1 - line // 2)
         return across + odd, across + 1 - odd, line + 1 - 2 * odd, line
 
-    def by_size(self, body):
-        pl.when(self.odd == 0)(lambda: body(self.sz.big))
-        pl.when(self.odd == 1)(lambda: body(self.sz.small))
+    def owners(self, part, body):
+        if part == 0:
+            body()
+        else:
+            pl.when(self.odd == 0)(body)
 
     def local(self):
         local = self.links.local_sems.at[self.links.used_local]
@@ -413,54 +446,51 @@
         return local
 
     def to_owners(self, source, target):
+        return [self.part_to_owners(source, target, part) for part in range(2)]
+
+    def part_to_owners(self, source, target, part):
         sz, links = self.sz, self.links
         pair, local = links.pair(), self.local()
-
-        def own(size):
-            pltpu.make_async_copy(
-                source.at[self.channels(links.row, links.col, size)],
-                target.at[self.block(self.token, size)],
-                local,
-            ).start()
-
-        self.by_size(own)
-        half = sz.peers * sz.hid // 2
-        first = (links.plane // 2) * sz.hid + links.col
+        there = target.at[part, self.block(self.token)]
+
+        def own():
+            mine = source.at[self.channels(links.row, links.col, part)]
+            pltpu.make_async_copy(mine, there, local).start()
+
+        self.owners(part, own)
+        apart = 1 + part
+        devices = sz.peers * sz.hid // apart
+        first = (links.plane // apart) * sz.hid + links.col
 
         for turn, line in enumerate(self.far_first()):
 
             def post(step, carry):
-                index = lax.rem(first + step, half)
-                col = lax.rem(index, sz.hid)
-                for odd, size in ((0, sz.big), (1, sz.small)):
-                    row = line * sz.peers + 2 * (index // sz.hid) + odd
-
-                    def send():
-                        links.copy(
-                            source.at[self.channels(row, col, size)],
-                            target.at[self.block(self.token, size)],
-                            pair,
-                            row,
-                            col,
-                        ).start()
-
-                    if turn < sz.group - 1:
-                        send()
-                    else:
-                        pl.when((step > 0) | (self.odd != odd))(send)
+                index = lax.rem(first + step, devices)
+                row, col = line * sz.peers + apart * (index // sz.hid), lax.rem(index, sz.hid)
+                piece = source.at[self.channels(row, col, part)]
+                links.copy(piece, there, pair, row, col).start()
                 return carry
 
-            lax.fori_loop(0, half, post, 0)
+            if turn < sz.group - 1:
+                lax.fori_loop(0, devices, post, 0)
+            else:
+                lax.fori_loop(1, devices, post, 0)
+                if part == 1:
+
+                    @pl.when(self.odd == 1)
+                    def _():
+                        post(0, 0)
+
         return pair, local
 
-    def to_tokens(self, source, target):
+    def to_tokens(self, source, target, part):
         sz, links = self.sz, self.links
         pair, local = links.pair(), self.local()
-
-        def send(size):
-            mine = target.at[self.channels(links.row, links.col, size)]
-            pltpu.make_async_copy(source.at[self.block(self.token, size)], mine, local).start()
-
+        there = target.at[self.channels(links.row, links.col, part)]
+
+        def send():
+            mine = source.at[part, self.block(self.token)]
+            pltpu.make_async_copy(mine, there, local).start()
             devices = sz.peers * sz.hid
             first = links.plane * sz.hid + links.col
 
@@ -469,37 +499,49 @@
                 def post(step, carry):
                     index = lax.rem(first + step, devices)
                     row, col = line * sz.peers + index // sz.hid, lax.rem(index, sz.hid)
-                    peer = row * sz.hid + col
-                    links.copy(source.at[self.block(peer, size)], mine, pair, row, col).start()
+                    piece = source.at[part, self.block(row * sz.hid + col)]
+                    links.copy(piece, there, pair, row, col).start()
                     return carry
 
                 lax.fori_loop(0 if turn < sz.group - 1 else 1, devices, post, 0)
 
-        self.by_size(send)
+        self.owners(part, send)
         return pair, local
 
-    def wait(self, tokens, by_tokens, by_owners, sent_by_tokens):
+    def wait(self, tokens, part, flat, sent_to_owners):
         sz, links = self.sz, self.links
         pair, local = tokens
-
-        def wait(size):
-            first = by_owners.at[pl.ds(0, size)]
-            pltpu.make_async_copy(first, first, local).wait()
-            all_tokens = by_owners.at[pl.ds(0, (sz.count - 1) * size)]
-            all_channels = by_tokens.at[pl.ds(0, sz.width - size)]
-            sent, came = all_tokens, all_channels
-            if sent_by_tokens:
-                sent, came = came, sent
-            links.copy(came, came, pair, links.row, 1 - links.col).wait_recv()
-            links.copy(sent, sent, pair, links.row, 1 - links.col).wait_send()
-
-        self.by_size(wait)
-
-    def owners_wait(self, tokens, source, target):
-        self.wait(tokens, source, target, True)
-
-    def tokens_wait(self, tokens, source, target):
-        self.wait(tokens, target, source, False)
+        rows = lambda count: flat.at[pl.ds(0, count * 16)]
+        all_devices = sz.count - 1
+
+        def owner_side():
+            pltpu.make_async_copy(rows(1), rows(1), local).wait()
+            copy = links.copy(rows(all_devices), rows(all_devices), pair, links.row, 1 - links.col)
+            if sent_to_owners:
+                copy.wait_recv()
+            else:
+                copy.wait_send()
+
+        def token_side(count):
+            copy = links.copy(rows(count), rows(count), pair, links.row, 1 - links.col)
+            if sent_to_owners:
+                copy.wait_send()
+            else:
+                copy.wait_recv()
+
+        self.owners(part, owner_side)
+        if part == 0:
+            token_side(all_devices)
+        else:
+            pl.when(self.odd == 0)(lambda: token_side(sz.count // 2 - 1))
+            pl.when(self.odd == 1)(lambda: token_side(sz.count // 2))
+
+    def owners_wait(self, tokens, part, target):
+        self.wait(tokens[part], part, target.at[0], True)
+
+    def tokens_wait(self, tokens, source):
+        for part in range(2):
+            self.wait(tokens[part], part, source.at[0], False)
 
 
 CHUNK = 8
@@ -509,14 +551,14 @@
     return pl.ds(pl.multiple_of(index * size, size), size)
 
 
-def dft(sz, b, source, base, stride, target, unroll=2):
+def dft(sz, b, source, base, stride, target, first=0, chunks=4, unroll=2):
     steps, outer = sz.steps, sz.outer
 
     def chunk(index, carry):
         cos = b.twist[:, :LANES]
         sin = b.twist[:, LANES:]
         for line in range(CHUNK):
-            start = base + index * CHUNK + line
+            start = base + (index - first) * CHUNK + line
             b.wide[:, line * LANES : (line + 1) * LANES] = source[
                 pl.ds(start, steps, stride=stride), :
             ].astype(BF16)
@@ -531,10 +573,10 @@
         target[place(index, CHUNK * outer), :] = nn(b.turned[...], b.inner_fwd[...])
         return carry
 
-    lax.fori_loop(0, sz.big // CHUNK, chunk, 0, unroll=unroll)
-
-
-def inverse_dft(sz, b, target, base, stride, unroll=2):
+    lax.fori_loop(first, first + chunks, chunk, 0, unroll=unroll)
+
+
+def inverse_dft(sz, b, target, base, stride, first=0, chunks=4, unroll=2):
     steps, outer = sz.steps, sz.outer
 
     def chunk(index, carry):
@@ -550,13 +592,13 @@
             b.mid_half[outer : 2 * outer, lanes] = (imag * cos + real * sin).astype(BF16)
         value = nn(b.outer_inv[...], b.mid_half[...])
         for line in range(CHUNK):
-            start = base + index * CHUNK + line
+            start = base + (index - first) * CHUNK + line
             target[pl.ds(start, steps, stride=stride), :] = value[
                 :, line * LANES : (line + 1) * LANES
             ]
         return carry
 
-    lax.fori_loop(0, sz.big // CHUNK, chunk, 0, unroll=unroll)
+    lax.fori_loop(first, first + chunks, chunk, 0, unroll=unroll)
 
 
 def first_channel(sz):
@@ -617,7 +659,7 @@
     spec = b.filt_spec[layer]
     span = sz.big * outer
     for way in range(2):
-        dft(sz, b, b.tall, way * piece, 2 * piece, b.spec)
+        dft(sz, b, b.tall, way * piece, 2 * piece, b.spec, unroll=1)
         if way == 0:
             spec[...] = b.spec[0:span, :].astype(BF16)
         else:
@@ -625,36 +667,32 @@
             spec[:, LANES:] = (spec[:, LANES:].astype(F32) - b.spec[0:span, LANES:]).astype(BF16)
 
 
-def conv_forward(sz, b, layer, landed):
-    b.tall[0 : sz.count * sz.big, :] = landed[...].astype(F32)
-    dft(sz, b, b.tall, 0, sz.big, b.spec, True)
-    span = sz.big * sz.outer
+def convolve(sz, b, layer, landed, part, back):
+    count = 16 // CHUNK
+    b.tall[0 : sz.count * 16, :] = landed[part].astype(F32)
+    dft(sz, b, b.tall, 0, 16, b.spec, part * count, count, True)
     filt = b.filt_spec[layer]
-    for seq in range(sz.seqs):
-        rows = slice(seq * span, (seq + 1) * span)
-        re, im = b.spec[rows, :LANES], b.spec[rows, LANES:]
+    rows = slice(part * 16 * sz.outer, (part + 1) * 16 * sz.outer)
+    re, im = b.spec[rows, :LANES], b.spec[rows, LANES:]
+    fil_re, fil_im = filt[rows, :LANES].astype(F32), filt[rows, LANES:].astype(F32)
+    if back:
+        b.flat[rows, :LANES] = (re * fil_re + im * fil_im).astype(BF16)
+        b.flat[rows, LANES:] = (im * fil_re - re * fil_im).astype(BF16)
+    else:
         b.sig_spec[layer][rows, :LANES] = re.astype(BF16)
         b.sig_spec[layer][rows, LANES:] = im.astype(BF16)
-        fil_re, fil_im = filt[:, :LANES].astype(F32), filt[:, LANES:].astype(F32)
         b.flat[rows, :LANES] = (re * fil_re - im * fil_im).astype(BF16)
         b.flat[rows, LANES:] = (re * fil_im + im * fil_re).astype(BF16)
-    inverse_dft(sz, b, b.tall, 0, sz.big, True)
-    b.staged[...] = b.tall[0 : sz.count * sz.big, :].astype(BF16)
-
-
-def conv_backward(sz, b, layer, landed):
-    b.tall[0 : sz.count * sz.big, :] = landed[...].astype(F32)
-    dft(sz, b, b.tall, 0, sz.big, b.spec, True)
-    span = sz.big * sz.outer
-    filt = b.filt_spec[layer]
-    for seq in range(sz.seqs):
-        rows = slice(seq * span, (seq + 1) * span)
-        re, im = b.spec[rows, :LANES], b.spec[rows, LANES:]
-        fil_re, fil_im = filt[:, :LANES].astype(F32), filt[:, LANES:].astype(F32)
-        b.flat[rows, :LANES] = (re * fil_re + im * fil_im).astype(BF16)
-        b.flat[rows, LANES:] = (im * fil_re - re * fil_im).astype(BF16)
-    inverse_dft(sz, b, b.tall, 0, sz.big, True)
-    b.staged[...] = b.tall[0 : sz.count * sz.big, :].astype(BF16)
+    inverse_dft(sz, b, b.tall, 0, 16, part * count, count, True)
+    b.staged[part] = b.tall[0 : sz.count * 16, :].astype(BF16)
+
+
+def conv_forward(sz, b, layer, landed, part):
+    convolve(sz, b, layer, landed, part, False)
+
+
+def conv_backward(sz, b, layer, landed, part):
+    convolve(sz, b, layer, landed, part, True)
 
 
 def taps_gradient(sz, b, layer, landed, signal):
@@ -673,7 +711,7 @@
     for way in range(2):
         b.flat[0:span, :LANES] = total_re.astype(BF16)
         b.flat[0:span, LANES:] = (total_im if way == 0 else -total_im).astype(BF16)
-        inverse_dft(sz, b, b.tall, way * piece, 2 * piece)
+        inverse_dft(sz, b, b.tall, way * piece, 2 * piece, unroll=True)
     taps = own_taps(sz, b.filters[layer])
     count = 4
 
@@ -691,13 +729,18 @@
     start = jnp.zeros((2 * piece, ORDER), F32)
     total = lax.fori_loop(0, sz.steps // count, chunk, start, unroll=2)
 
-    def product(block, products):
-        rows = place(block, piece)
-        return products + landed[rows, :].astype(F32) * signal[rows, :].astype(F32)
-
-    start = jnp.zeros((piece, LANES), F32)
-    products = lax.fori_loop(0, sz.count, product, start, unroll=8)
-    column = jnp.sum(products, axis=1, keepdims=True)
+    columns = []
+    for part in range(2):
+
+        def product(block, products):
+            rows = place(block, 16)
+            here = landed[part, rows, :].astype(F32)
+            return products + here * signal[part, rows, :].astype(F32)
+
+        start = jnp.zeros((16, LANES), F32)
+        products = lax.fori_loop(0, sz.count, product, start, unroll=4)
+        columns.append(jnp.sum(products, axis=1, keepdims=True))
+    column = jnp.concatenate(columns, axis=0)
     row = jnp.transpose(jnp.broadcast_to(column, (piece, LANES)))[0:8, :]
     b.taps_work[...] = jnp.zeros_like(b.taps_work)
     b.taps_work[0 : sz.big, :] = total[0 : sz.big, :]
@@ -725,15 +768,6 @@
         rows = block_of(sz, block)
         middle[:, rows] = tn(mixed[rows, :], b.mixer[layer, 2, block])
     middle[...] = middle[...] + b.stream[layer][...]
-
-
-def mixer_gradient(sz, b, kind_row, values, mine, give):
-    low = lax.axis_index("hid") == 0
-    left = jnp.concatenate(values[: sz.side_blocks], axis=1)
-    right = jnp.concatenate(values[sz.side_blocks :], axis=1)
-    rows = slice(kind_row * sz.size, (kind_row + 1) * sz.size)
-    mine[rows, :] = jnp.where(low, left, right).astype(BF16)
-    give[rows, :] = jnp.where(low, right, left).astype(BF16)
 
 
 def gain_gradient(sz, b, row, value, mine, give):
@@ -896,7 +930,6 @@
 def layout(sz):
     layers, own, width = sz.layers, sz.own, sz.width
     wide = 2 * sz.big * sz.steps
-    late = sz.late_rows * sz.rows
     per_layer = dict(
         stream=((own, width), F32),
         normed=((own, width), BF16),
@@ -910,9 +943,9 @@
         skip=((width, LANES), F32),
         filt_spec=((sz.big * sz.outer, 2 * LANES), BF16),
         sig_spec=((sz.pairs * sz.outer, 2 * LANES), BF16),
-        fore_in=((sz.count * sz.big, LANES), BF16),
+        fore_in=((2, sz.count * 16, LANES), BF16),
         fore_out=((width, own), BF16),
-        back_in=((sz.count * sz.big, LANES), BF16),
+        back_in=((2, sz.count * 16, LANES), BF16),
         back_out=((width, own), BF16),
         plane_first=((3, 2, 2, sz.group // 2, sz.deep, sz.part), BF16),
         plane_give=((3, 2, sz.group // 2, sz.deep, sz.part), BF16),
@@ -943,7 +976,7 @@
         mid_half=((2 * sz.outer, CHUNK * LANES), BF16),
         spec=((sz.pairs * sz.outer, 2 * LANES), F32),
         conv_grad=((width, own), BF16),
-        staged=((sz.count * sz.big, LANES), BF16),
+        staged=((2, sz.count * 16, LANES), BF16),
         grad_middle=((own, width), F32),
         grad_o=((own, width), BF16),
         gate_grad=((width, own), BF16),
@@ -959,16 +992,11 @@
         taps_work=((sz.taps_rows, ORDER), F32),
         gain_mine=((16, sz.half), F32),
         gain_give=((16, sz.half), F32),
+        late_parts=((sz.peers, sz.group, sz.deeps[1], sz.half), BF16),
         late_gain_mine=((16, sz.half), F32),
         late_gain_give=((16, sz.half), F32),
-        late_mine=((late, sz.half), BF16),
-        late_give=((late, sz.half), BF16),
-        late_got=((late, sz.half), BF16),
-        late_in=((sz.rows, sz.late_rows, sz.half), BF16),
-        late_sum=((sz.late_rows, sz.half), BF16),
         out_keep=((2, own, sz.half), BF16),
         taps_line=((layers, sz.group, sz.taps_rows, ORDER), BF16),
-        late_out=((sz.late_rows, sz.half), BF16),
     )
     names, specs = [], []
     for name, (shape, kind) in per_layer.items():
@@ -991,7 +1019,7 @@
 
 TABLES = ("pos", "outer_fwd", "outer_inv", "inner_fwd", "inner_inv", "twist")
 INPUTS = ("hidden_in", "d_out", "gains", "mixer", "skip", "filters", "gate_up", "down") + TABLES
-OUTPUTS = ("hidden_out", "grad_in", "upper", "lower", "late", "taps", "units")
+OUTPUTS = ("hidden_out", "grad_in", "early", "late", "taps", "units")
 
 
 def program_kernel(sz, *refs):
@@ -1175,13 +1203,15 @@
             for each in range(sz.layers):
                 row = b.skip_rows[each : each + 1, :]
                 b.skip[each][...] = jnp.transpose(jnp.broadcast_to(row, (LANES, sz.width)))
-        exchange.owners_wait(moving, b.inner[layer], b.fore_in[layer])
+        returning = []
+        for part in range(2):
+            exchange.owners_wait(moving, part, b.fore_in[layer])
+            conv_forward(sz, b, layer, b.fore_in[layer], part)
+            returning.append(exchange.to_tokens(b.staged, b.fore_out[layer], part))
         if layer == 0:
             top_grads.step(1)
         else:
             top_grads.rest()
-        conv_forward(sz, b, layer, b.fore_in[layer])
-        moving = exchange.to_tokens(b.staged, b.fore_out[layer])
         if layer == 0:
             both("out_mixer")
             if sz.layers > 1:
@@ -1195,7 +1225,7 @@
         done(loads["down", layer])
         if layer == 0:
             top_grads.step(2)
-        exchange.tokens_wait(moving, b.staged, b.fore_out[layer])
+        exchange.tokens_wait(returning, b.staged)
         mix(sz, b, layer, b.fore_out[layer])
         norm_to(b.middle[layer][...], b.nbuf[layer].at[slots(0, 1)], layer, 1)
         normed_parts.append(Gather(b.nbuf[layer]))
@@ -1225,9 +1255,9 @@
     gain_grad = mixer_backward(sz, b, top, grad_next, total)
     moving = exchange.to_owners(b.conv_grad, b.back_in[top])
     gain_gradient(sz, b, 2 * top, gain_grad, b.gain_mine, b.gain_give)
-    upper = Payload(sz, b, links, 0, outputs["upper"])
-    lower = Payload(sz, b, links, 1, outputs["lower"])
-    upper.matrix(0, out_gradient(sz, b, top))
+    early = Payload(sz, b, links, 0, outputs["early"])
+    late = Payload(sz, b, links, 1, outputs["late"])
+    early.matrix(0, out_gradient(sz, b, top))
     done(out_moving)
     value = b.middle[top][...] + b.out_sum[0:own, :] + b.out_got[top][...].astype(F32)
     value = value.astype(BF16)
@@ -1269,14 +1299,20 @@
             pair = links.in_line(part, target)
             units_moving.append((layer, kind, pair))
 
-    exchange.owners_wait(moving, b.conv_grad, b.back_in[top])
-    conv_backward(sz, b, top, b.back_in[top])
-    moving = exchange.to_tokens(b.staged, b.back_out[top])
+    def convolve_back(layer):
+        returning = []
+        for part in range(2):
+            exchange.owners_wait(moving, part, b.back_in[layer])
+            conv_backward(sz, b, layer, b.back_in[layer], part)
+            returning.append(exchange.to_tokens(b.staged, b.back_out[layer], part))
+        return returning
+
+    moving = convolve_back(top)
     normed_parts[top].rest()
     normed_parts[0].step(0)
     normed_parts[top].finish()
     plane_moving[top] = ff_gradients(sz, b, top, links)
-    exchange.tokens_wait(moving, b.staged, b.back_out[top])
+    exchange.tokens_wait(moving, b.staged)
     value, gain_grad = input_backward(sz, b, top, b.back_out[top])
     b.out_sum[0:own, :] = value
     b.gbuf[0][0:own, :] = value.astype(BF16)
@@ -1285,9 +1321,8 @@
     gather.step(0)
     normed_parts[0].step(1)
     gain_gradient(sz, b, 2 * top - 1, gain_grad, b.gain_mine, b.gain_give)
-    upper.matrix(1, in_gradient(sz, b, top, b.inner_grad))
-    upper.matrix(2, in_gradient(sz, b, top, b.gate_grad))
-    upper.to_partner()
+    early.matrix(1, in_gradient(sz, b, top, b.inner_grad))
+    early.matrix(2, in_gradient(sz, b, top, b.gate_grad))
     done(near)
     ff_backward(sz, b, 0, False)
     b.sum_give[...] = b.grad_sum[own:, :].astype(BF16)
@@ -1300,77 +1335,55 @@
 
     moving = exchange.to_owners(b.conv_grad, b.back_in[0])
     units_middle(top)
-    upper.to_plane()
+    gain_gradient(sz, b, 0, gain_grad, b.gain_mine, b.gain_give)
+    early.matrix(3, out_gradient(sz, b, 0))
+    early.matrix(4, in_gradient(sz, b, 0, b.gate_grad))
+    early.rows16(5, b.gain_mine[...], b.gain_give[...])
+    early.to_partner()
     taps_to_line(top)
-    gain_gradient(sz, b, 0, gain_grad, b.gain_mine, b.gain_give)
-    lower.matrix(0, out_gradient(sz, b, 0))
-    lower.matrix(1, in_gradient(sz, b, 0, b.gate_grad))
-    lower.rows16(2, b.gain_mine[...], b.gain_give[...])
-    lower.to_partner()
     gather.step(2)
-    exchange.owners_wait(moving, b.conv_grad, b.back_in[0])
-    lower.to_plane()
-    conv_backward(sz, b, 0, b.back_in[0])
-    moving = exchange.to_tokens(b.staged, b.back_out[0])
+    early.to_plane()
+    moving = convolve_back(0)
     units_end(top)
     normed_parts[0].rest()
     gather.rest()
-    upper.middle()
     taps_to_plane(top)
     normed_parts[0].finish()
     gather.finish()
-    between = (lower.middle, upper.to_line, None)
+    between = (early.middle, None, None)
     plane_moving[0] = ff_gradients(sz, b, 0, links, between)
-    exchange.tokens_wait(moving, b.staged, b.back_out[0])
+    exchange.tokens_wait(moving, b.staged)
     value, gain_grad = input_backward(sz, b, 0, b.back_out[0])
 
     left, right = value[:, : sz.half], value[:, sz.half :]
     keep, give = b.out_sum.at[0:own, 0 : sz.half], b.out_sum.at[own:, 0 : sz.half]
     keep[...] = jnp.where(low, left, right)
     give[...] = jnp.where(low, right, left)
-    mixer_gradient(sz, b, 0, in_gradient(sz, b, 0, b.inner_grad), b.late_mine, b.late_give)
+    late.matrix(0, in_gradient(sz, b, 0, b.inner_grad))
     gain_gradient(sz, b, 0, gain_grad, b.late_gain_mine, b.late_gain_give)
-    rows = slice(sz.size, sz.size + 16)
-    b.late_mine[rows, :] = b.late_gain_mine[...].astype(BF16)
-    b.late_give[rows, :] = b.late_gain_give[...].astype(BF16)
-    last = slice(sz.size + 16, sz.rows * sz.late_rows)
-    b.late_mine[last, :] = jnp.zeros_like(b.late_mine[last, :])
-    b.late_give[last, :] = jnp.zeros_like(b.late_give[last, :])
-    late_pair = links.sibling(b.late_give, b.late_got)
+    late.rows16(1, b.late_gain_mine[...], b.late_gain_give[...])
+    late.to_partner()
     place = outputs["grad_in"].at[mine_rows]
     ending += [links.load(keep, place), links.sibling(give, place)]
 
-    done(late_pair)
-    b.late_mine[...] = (b.late_mine[...].astype(F32) + b.late_got[...].astype(F32)).astype(BF16)
-    few = lambda index: pl.ds(pl.multiple_of(index * sz.late_rows, sz.late_rows), sz.late_rows)
-    rows_pair = links.in_rows(
-        lambda member: b.late_mine.at[few(member)], b.late_in.at[links.row]
-    )
-    lower.to_line()
-    units_middle(0, (0, 1))
+    early.to_line()
+    late.to_plane()
+    units_middle(0, (0,))
+    early.back_line()
     taps_to_line(0)
+    late.to_line()
+    units_middle(0, (1,))
+    early.back_plane()
     units_middle(0, (2,))
-    upper.back_line()
-    lower.back_line()
+    late.back_line()
     units_end(0, (0,))
-    links.wait(rows_pair, b.late_in.at[pl.ds(0, sz.rows - 1)])
-    b.late_in[links.row] = b.late_mine[few(links.row), :]
-    late = outputs["late"]
-    b.late_out[...] = jnp.sum(b.late_in[...].astype(F32), axis=0).astype(BF16)
-    place = late.at[few(links.row)]
-    ending.append(links.load(b.late_out, place))
-    spread_rows = links.in_rows(lambda member: b.late_out, place)
-    units_end(0, (1,))
-    upper.back_plane()
-    units_end(0, (2,))
-    lower.back_plane()
-    upper.spread.middle()
-    lower.spread.middle()
+    early.spread.middle()
+    late.back_plane()
+    units_end(0, (1, 2))
     taps_to_plane(0)
-    ending += [upper.finish(), lower.finish()]
+    ending += [early.finish(), late.finish()]
     for layer, kind, pair in units_moving:
         links.wait(pair, outputs["units"].at[layer, kind, pl.ds(0, sz.group - 1)])
-    links.wait(spread_rows, late.at[pl.ds(0, (sz.rows - 1) * sz.late_rows)])
     for layer, pair in taps_moving.items():
         links.wait(pair, outputs["taps"].at[layer, pl.ds(0, sz.peers - 1)])
     for copy in ending:
@@ -1378,11 +1391,11 @@
 
 
 def results_kernel(sz, *refs):
-    raw, outs, scratch = refs[:7], refs[7:15], refs[15:]
-    targets, held = scratch[:7], scratch[7:15]
+    raw, outs, scratch = refs[:6], refs[6:14], refs[14:]
+    targets, held = scratch[:6], scratch[6:14]
     hidden_out, grad_in, gain_out, mixer_out, skip_out, taps_out, pair_out, down_out = held
-    upper, lower, late, taps, units = targets[2:]
-    channels, sems = scratch[15:]
+    early, late, taps, units = targets[2:]
+    channels, sems = scratch[14:]
     targets = (hidden_out, grad_in) + targets[2:]
     copies = [
         pltpu.make_async_copy(source, target, sems.at[index])
@@ -1398,7 +1411,7 @@
         leaving.append(copy)
 
     layers = sz.layers
-    copies[6].wait()
+    copies[5].wait()
     for kind in range(3):
         for layer in range(layers):
             for line in range(sz.group):
@@ -1410,7 +1423,7 @@
                     down_out[layer, :, lanes] = value
     leave(6)
     leave(7)
-    copies[5].wait()
+    copies[4].wait()
     for layer in range(layers):
         for way in range(3):
             for row in range(sz.rows):
@@ -1430,7 +1443,7 @@
                 skip_out[layer : layer + 1, :] = turned[0:1, :]
     leave(4)
     leave(5)
-    for copy in copies[2:5]:
+    for copy in copies[2:4]:
         copy.wait()
 
     def matrix(payload, place, layer, kind):
@@ -1444,16 +1457,16 @@
                     :, block_of(sz, block)
                 ]
 
-    for place, kind in enumerate((2, 0, 1)):
-        matrix(upper, place, 1, kind)
-    for place, kind in enumerate((2, 1)):
-        matrix(lower, place, 0, kind)
-    rows = late[0 : sz.size, :].astype(F32)
-    for block in range(sz.side_blocks):
-        mixer_out[0, 0, block] = rows[:, block_of(sz, block)]
-    index = 2 * (sz.size // sz.deeps[1])
-    gains = lower[index // sz.group, index % sz.group].astype(F32)
-    gain_out[0, 0:1, :] = late[sz.size : sz.size + 16, :].astype(F32)[0:1, :]
+    for place, (layer, kind) in enumerate(((1, 2), (1, 0), (1, 1), (0, 2), (0, 1))):
+        matrix(early, place, layer, kind)
+    matrix(late, 0, 0, 0)
+
+    def gain_rows(payload, place):
+        index = place * (sz.size // payload.shape[2])
+        return payload[index // sz.group, index % sz.group].astype(F32)
+
+    gains = gain_rows(early, 5)
+    gain_out[0, 0:1, :] = gain_rows(late, 1)[0:1, :]
     for row in range(1, 2 * layers):
         gain_out[row // 2, row % 2 : row % 2 + 1, :] = gains[row - 1 : row, :]
     leave(2)
@@ -1498,7 +1511,6 @@
         ((2 * sz.own, sz.half), F32),
         ((sz.peers, sz.group, sz.deeps[0], sz.half), BF16),
         ((sz.peers, sz.group, sz.deeps[1], sz.half), BF16),
-        ((sz.rows * sz.late_rows, sz.half), BF16),
         ((sz.layers, sz.peers, sz.group, sz.taps_rows, ORDER), BF16),
         ((sz.layers, 3, sz.group, sz.deep, sz.part), BF16),
     )

time: 164 us -> 161 us (0.982)
  Pallas kernels: 163 us -> 160 us
    pallas_call x1, Pallas kernels: 159 us -> 156 us  [program(): pl.pallas_call(functools.partial(program_kernel, sz), out_shape=tuple((ja...]
where the time goes in v1:
time: 161 us
  Pallas kernels  160 us (99%)
    pallas_call x1, Pallas kernels, program(): pl.pallas_call(functools.partial(program_kernel, sz), out_shape=tuple((ja...  156 us
    pallas_call x1, Pallas kernels, results(): pl.pallas_call(functools.partial(results_kernel, sz), out_shape=tuple((ja...  4.12 us

profile of v1, /device:TPU:0, one launch (start us, length us, event | category | flops | bytes accessed | tf_op | source)
XLA Modules:
  0.0 160.9 jit_solution(10951160560493249822)
XLA Ops:
  0.6 155.9 %program.1 = (bf16[256,384]{1,0:T(8,128)(2,1)}, f32[256,384]{1,0:T(8,128)}, bf16[4,4,64,384]{3,2,1,0:T(8,128)(2,1)}, bf16[4,4,16,384]{3,2,1,0:T(8,128)(2,1)}, bf...) custom-call(bf16[256,384]{1,0:T(8,128)(2,1)} %refs_0_.1, bf16[256,384]{1,0:T(8,128)(2,1)} %refs_1_.1, ...), custom_call_target="tpu_custom_call" | custom-call | tf_op jit(solution)/shard_map/program/pallas_call | solution.py:1517
  156.5 4.1 %results.1 = (bf16[256,384]{1,0:T(8,128)(2,1)}, f32[256,384]{1,0:T(8,128)}, f32[2,2,384]{2,1,0:T(2,128)}, f32[2,3,2,192,192]{4,3,2,1,0:T(8,128)}, f32[2,384]{1,0...) custom-call(bf16[256,384]{1,0:T(8,128)(2,1)} %get-tuple-element.14.refs_0_, ...), custom_call_target="tpu_custom_call" | custom-call | tf_op jit(solution)/shard_map/results/pallas_call | solution.py:1494

commit v2 on v1

--- a/solution.py
+++ b/solution.py
@@ -968,7 +968,7 @@
         up=((layers, 2, width, sz.units), BF16),
         down=((layers, width, sz.units), BF16),
         env=((2 * sz.big, sz.length), F32),
-        tall=((max(wide, sz.count * sz.big), LANES), F32),
+        tall=((max(wide, sz.count * sz.big) + 2 * sz.big, LANES), F32),
         wide=((sz.steps, CHUNK * LANES), BF16),
         turned=((CHUNK * sz.outer, 2 * LANES), BF16),
         mid=((2 * sz.outer, CHUNK * LANES), F32),

time: 161 us -> 161 us (level)
  no operation moved by 1% of the time
where the time goes in v2:
time: 161 us
  Pallas kernels  160 us (99%)
    pallas_call x1, Pallas kernels, program(): pl.pallas_call(functools.partial(program_kernel, sz), out_shape=tuple((ja...  156 us
    pallas_call x1, Pallas kernels, results(): pl.pallas_call(functools.partial(results_kernel, sz), out_shape=tuple((ja...  4.12 us

profile of v2, /device:TPU:0, one launch (start us, length us, event | category | flops | bytes accessed | tf_op | source)
XLA Modules:
  0.0 160.9 jit_solution(2267145863514707459)
XLA Ops:
  0.6 155.9 %program.1 = (bf16[256,384]{1,0:T(8,128)(2,1)}, f32[256,384]{1,0:T(8,128)}, bf16[4,4,64,384]{3,2,1,0:T(8,128)(2,1)}, bf16[4,4,16,384]{3,2,1,0:T(8,128)(2,1)}, bf...) custom-call(bf16[256,384]{1,0:T(8,128)(2,1)} %refs_0_.1, bf16[256,384]{1,0:T(8,128)(2,1)} %refs_1_.1, ...), custom_call_target="tpu_custom_call" | custom-call | tf_op jit(solution)/shard_map/program/pallas_call | solution.py:1517
  156.5 4.1 %results.1 = (bf16[256,384]{1,0:T(8,128)(2,1)}, f32[256,384]{1,0:T(8,128)}, f32[2,2,384]{2,1,0:T(2,128)}, f32[2,3,2,192,192]{4,3,2,1,0:T(8,128)}, f32[2,384]{1,0...) custom-call(bf16[256,384]{1,0:T(8,128)(2,1)} %get-tuple-element.14.refs_0_, ...), custom_call_target="tpu_custom_call" | custom-call | tf_op jit(solution)/shard_map/results/pallas_call | solution.py:1494
